TPU v7x, 32 devices: a whole 2x2x4 slice. The times are simulated.
32 devices in a mesh: dp: 4 (over x, core), seq: 8 (over z, y).
Axes of the slice: x: 2, y: 2, z: 4, core: 2. Of those that a mesh axis runs over, the one named last changes fastest.
Arguments:
- tokens: bfloat16 [16384, 768], P(('dp', 'seq')), may hold values from -6 to 6
- cotangent: bfloat16 [16384, 768], P(('dp', 'seq')), may hold values from -6 to 6
- document_bounds: int32 [4, 2], replicated, may hold values from 1 to 4095, as said below
- routes: int32 [3, 2048], P(None, ('dp', 'seq')), may hold values from -1 to 511, as said below
- attention_gain: float32 [768], replicated, may hold values from 0.5 to 1.5
- feedforward_gain: float32 [768], replicated, may hold values from 0.5 to 1.5
- router: float32 [3, 768], replicated, may hold values from -0.21875 to 0.21875
- light_query: bfloat16 [768, 768], replicated, may hold values from -0.3125 to 0.3125
- light_keyval: bfloat16 [768, 1536], replicated, may hold values from -0.21875 to 0.21875
- light_output: bfloat16 [768, 768], replicated, may hold values from -0.875 to 0.875
- heavy_query: bfloat16 [768, 768], replicated, may hold values from -0.3125 to 0.3125
- heavy_keyval: bfloat16 [768, 1536], replicated, may hold values from -0.21875 to 0.21875
- heavy_output_weight: bfloat16 [768, 768], replicated, may hold values from -0.875 to 0.875
- light_expand: bfloat16 [768, 2048], replicated, may hold values from -0.21875 to 0.21875
- light_reduce: bfloat16 [1024, 768], replicated, may hold values from -0.1875 to 0.1875
- heavy_expand: bfloat16 [768, 8192], replicated, may hold values from -0.21875 to 0.21875
- heavy_reduce: bfloat16 [4096, 768], replicated, may hold values from -0.09375 to 0.09375
Outputs:
- output: bfloat16 [16384, 768], P(('dp', 'seq'))
- tokens_grad: bfloat16 [16384, 768], P(('dp', 'seq'))
- attention_gain_grad: float32 [768], P('seq')
- feedforward_gain_grad: float32 [768], P('seq')
- router_grad: float32 [3, 768], P(None, 'seq')
- light_query_grad: float32 [768, 768], P('seq', 'dp')
- light_keyval_grad: float32 [768, 1536], P('seq', 'dp')
- light_output_grad: float32 [768, 768], P('seq', 'dp')
- heavy_query_grad: float32 [768, 768], P('seq', 'dp')
- heavy_keyval_grad: float32 [768, 1536], P('seq', 'dp')
- heavy_output_grad: float32 [768, 768], P('seq', 'dp')
- light_expand_grad: float32 [768, 2048], P('seq', 'dp')
- light_reduce_grad: float32 [1024, 768], P('seq', 'dp')
- heavy_expand_grad: float32 [768, 8192], P('seq', 'dp')
- heavy_reduce_grad: float32 [4096, 768], P('seq', 'dp')
Inputs may be any that keep to these rules, and one draw needn't show every extreme that they name: For each group, document_bounds holds (start, end) with 1 <= start <= 256 and 3840 <= end <= 4095. `routes`: within each block of 64 slots of a router the named tokens are distinct and come first, followed by -1 entries; each block names 32 to 64 tokens, and for each router some block names 64.
All inputs are finite; a program needn't handle non-finite values.
Results may differ from a plain program's by a relative error of at most 0.018.
Values may be sent and summed in bfloat16 or wider, within the bound.
No kernel may reach another device: no remote copies, remote signals or barrier semaphores. Data moves between devices by JAX's collectives and lax.ppermute only.
A program may use at most 320 MiB of HBM per device.

v0:
```python
import jax
import jax.numpy as jnp
from jax import lax
from jax.sharding import PartitionSpec as P

LH = 8
HHS = 64
WINDOW = 128


EPSILON = 1e-06
MASKED = -1e30
HIGHEST = lax.Precision.HIGHEST


def with_halo(cells, sides, width):
    for axis, dim in sides:
        count = lax.axis_size(axis)
        ends = count - 1
        head = lax.slice_in_dim(cells, 0, width, axis=dim)
        tail = lax.slice_in_dim(cells, cells.shape[dim] - width, cells.shape[dim], axis=dim)
        cells = jnp.concatenate(
            [
                lax.ppermute(tail, axis, [(i, (i + 1) % count) for i in range(ends)]),
                cells,
                lax.ppermute(head, axis, [((i + 1) % count, i) for i in range(ends)]),
            ],
            axis=dim,
        )
    return cells


def from_behind(block, axis, distance):
    devices = range(lax.axis_size(axis))
    route = [(i - distance, i) for i in devices if i - distance in devices]
    return lax.ppermute(block, axis, route)


def rms_norm(signal, scaling):
    return signal * lax.rsqrt(jnp.mean(signal * signal, -1, keepdims=True) + EPSILON) * scaling


def gated_gelu(paired):
    halfway = paired.shape[-1] // 2
    return jax.nn.gelu(paired[:, :halfway]) * paired[:, halfway:]


def segment_of(token_positions, bounds):
    return (token_positions >= bounds[0]).astype(jnp.int32) + (token_positions >= bounds[1]).astype(
        jnp.int32
    )


def matmul(former, latter):
    return jnp.dot(former, latter, preferred_element_type=jnp.float32)


def matmul_left(former, latter):
    return lax.dot_general(
        former, latter, (((0,), (0,)), ((), ())), preferred_element_type=jnp.float32
    )


def matmul_right(former, latter):
    return lax.dot_general(
        former, latter, (((1,), (1,)), ((), ())), preferred_element_type=jnp.float32
    )


def scatter_rows(chosen_row, slot_rows):
    return lax.dot_general(
        chosen_row.astype(jnp.float32), slot_rows, (((0,), (0,)), ((), ())), precision=HIGHEST
    )


def pick_values(chosen_row, token_values):
    return jnp.sum(jnp.where(chosen_row, token_values[None, :], 0.0), 1)


def pick_back(chosen_row, slot_values):
    return jnp.sum(jnp.where(chosen_row, slot_values[:, None], 0.0), 0)


def light_scores(queries, padded, offset, rows_block, leading_position, length, bounds):
    model_width = queries.shape[1]
    head_size = model_width // LH
    window_span = rows_block + 2 * WINDOW
    query_part = queries.reshape(rows_block, LH, head_size)
    key_part = padded[:, :model_width].reshape(window_span, LH, head_size)
    value_part = padded[:, model_width:].reshape(window_span, LH, head_size)
    scores = jnp.einsum(
        "qhd,khd->hqk", query_part, key_part, preferred_element_type=jnp.float32
    ) * head_size ** (-0.5)
    query_place = leading_position + offset + jnp.arange(rows_block, dtype=jnp.int32)
    key_place = leading_position + offset - WINDOW + jnp.arange(window_span, dtype=jnp.int32)
    allowed = (key_place[None, :] >= 0) & (key_place[None, :] < length)
    allowed = allowed & (jnp.abs(query_place[:, None] - key_place[None, :]) <= WINDOW)
    allowed = allowed & (
        segment_of(query_place, bounds)[:, None] == segment_of(key_place, bounds)[None, :]
    )
    return (scores, allowed, query_part, key_part, value_part)


def light_softmax(scores, allowed):
    masked = jnp.where(allowed[None], scores, MASKED)
    row_peak = jnp.max(masked, -1, keepdims=True)
    exponent = jnp.exp(masked - row_peak)
    row_total = jnp.sum(exponent, -1, keepdims=True)
    return (exponent / row_total, row_peak, row_total)


def heavy_softmax(scores, allowed):
    masked = jnp.where(allowed[None], scores, MASKED)
    row_peak = jnp.max(masked, -1, keepdims=True)
    exponent = jnp.where(allowed[None], jnp.exp(masked - row_peak), 0.0)
    row_total = jnp.sum(exponent, -1, keepdims=True)
    row_guard = jnp.where(row_total > 0, row_total, 1.0)
    return (exponent / row_guard, row_peak, row_guard)


def heavy_weights(scores, allowed, row_peak, row_guard):
    masked = jnp.where(allowed[None], scores, MASKED)
    return jnp.where(allowed[None], jnp.exp(masked - row_peak), 0.0) / row_guard


def head_slices(queries, keyvals, group_index, group_cols, heavy_width):
    column = group_index * group_cols
    heads_here = group_cols // HHS
    query_group = queries[:, column : column + group_cols].reshape(
        queries.shape[0], heads_here, HHS
    )
    key_group = keyvals[:, column : column + group_cols].reshape(keyvals.shape[0], heads_here, HHS)
    value_group = keyvals[:, heavy_width + column : heavy_width + column + group_cols].reshape(
        keyvals.shape[0], heads_here, HHS
    )
    return (query_group, key_group, value_group)


def softmax_back(weights, grad_part, value_part):
    grad_weights = jnp.einsum(
        "qhd,khd->hqk", grad_part, value_part, preferred_element_type=jnp.float32
    )
    inner = jnp.sum(weights * grad_weights, -1, keepdims=True)
    return ((weights * (grad_weights - inner)).astype(jnp.bfloat16), inner)


def key_side(
    query_rows,
    grad_rows,
    peaks,
    guards,
    inners,
    query_segment,
    key_rows,
    key_places,
    bounds,
    head_groups,
    group_cols,
    heavy_width,
    heavy_scale,
):
    row_count = key_rows.shape[0]
    query_count = query_rows.shape[0]
    heads_here = group_cols // HHS
    allowed_part = (key_places[None, :] >= 0) & (
        query_segment[:, None] == segment_of(key_places, bounds)[None, :]
    )
    key_parts = []
    value_parts = []
    for group_index in range(head_groups):
        query_group, key_group, value_group = head_slices(
            query_rows, key_rows, group_index, group_cols, heavy_width
        )
        scores = (
            jnp.einsum("qhd,khd->hqk", query_group, key_group, preferred_element_type=jnp.float32)
            * heavy_scale
        )
        weights = heavy_weights(scores, allowed_part, peaks[group_index], guards[group_index])
        grad_group = grad_rows[
            :, group_index * group_cols : (group_index + 1) * group_cols
        ].reshape(query_count, heads_here, HHS)
        grad_weights = jnp.einsum(
            "qhd,khd->hqk", grad_group, value_group, preferred_element_type=jnp.float32
        )
        grad_scores = (weights * (grad_weights - inners[group_index])).astype(jnp.bfloat16)
        key_parts.append(
            (
                jnp.einsum(
                    "hqk,qhd->khd", grad_scores, query_group, preferred_element_type=jnp.float32
                )
                * heavy_scale
            ).reshape(row_count, group_cols)
        )
        value_parts.append(
            jnp.einsum(
                "hqk,qhd->khd",
                weights.astype(jnp.bfloat16),
                grad_group,
                preferred_element_type=jnp.float32,
            ).reshape(row_count, group_cols)
        )
    return jnp.concatenate(key_parts + value_parts, 1)


def on_device(
    tokens,
    cotangent,
    document_bounds,
    routes,
    attention_gain,
    feedforward_gain,
    router,
    light_query,
    light_keyval,
    light_output,
    heavy_query,
    heavy_keyval,
    heavy_output_weight,
    light_expand,
    light_reduce,
    heavy_expand,
    heavy_reduce,
):
    tok_rows, model_width = tokens.shape
    slot_rows = routes.shape[1]
    heavy_width = heavy_query.shape[1]
    leading_position = lax.axis_index("seq") * tok_rows
    length = tok_rows * lax.axis_size("seq")
    bounds = lax.dynamic_index_in_dim(document_bounds, lax.axis_index("dp"), 0, keepdims=False)
    rows_block = min(512, tok_rows)
    window_span = rows_block + 2 * WINDOW
    light_size = model_width // LH
    group_cols = 4 * HHS
    heads_here = group_cols // HHS
    head_groups = heavy_width // group_cols
    heavy_scale = HHS ** (-0.5)
    inputs = tokens.astype(jnp.float32)
    normed_mixer = rms_norm(inputs, attention_gain)
    attention_lower = normed_mixer.astype(jnp.bfloat16)
    query_light = matmul(attention_lower, light_query).astype(jnp.bfloat16)
    keyval_light = matmul(attention_lower, light_keyval).astype(jnp.bfloat16)
    padded = with_halo(keyval_light, (("seq", 0),), WINDOW)
    offset = 0
    scores, allowed, query_part, key_part, value_part = light_scores(
        query_light, padded, offset, rows_block, leading_position, length, bounds
    )
    weights, row_peak, row_total = light_softmax(scores, allowed)
    light_parts = jnp.einsum(
        "hqk,khd->qhd", weights.astype(jnp.bfloat16), value_part, preferred_element_type=jnp.float32
    ).reshape(rows_block, model_width)
    light_stats = [(row_peak, row_total)]
    attended = light_parts.astype(jnp.bfloat16)
    residual = inputs + matmul(attended, light_output)
    alive_flags = routes >= 0
    lanes = jnp.arange(tok_rows, dtype=jnp.int32)
    chosen = routes[:, :, None] == lanes[None, None, :]
    chosen_low = chosen.astype(jnp.bfloat16)
    score_query = jax.nn.sigmoid(
        pick_values(chosen[0], jnp.dot(normed_mixer, router[0], precision=HIGHEST))
    )
    score_keyval = jax.nn.sigmoid(
        pick_values(chosen[1], jnp.dot(normed_mixer, router[1], precision=HIGHEST))
    )
    query_row_index = matmul(chosen_low[0], attention_lower).astype(jnp.bfloat16)
    keyvalue_row_index = matmul(chosen_low[1], attention_lower).astype(jnp.bfloat16)
    query_heavy = matmul(query_row_index, heavy_query).astype(jnp.bfloat16)
    raw_keyval = matmul(keyvalue_row_index, heavy_keyval)
    keyval_heavy = jnp.concatenate(
        [raw_keyval[:, :heavy_width], score_keyval[:, None] * raw_keyval[:, heavy_width:]], 1
    ).astype(jnp.bfloat16)
    slot_token_positions = jnp.where(alive_flags, leading_position + routes, -1)
    gathered_keyval, gathered_places = (
        lax.all_gather(keyval_heavy, "seq", axis=0, tiled=True),
        lax.all_gather(slot_token_positions[1], "seq", axis=0, tiled=True),
    )
    query_segment = segment_of(slot_token_positions[0], bounds)
    heavy_allowed = (gathered_places[None, :] >= 0) & (
        query_segment[:, None] == segment_of(gathered_places, bounds)[None, :]
    )
    heavy_parts = []
    heavy_stats = []
    for group_index in range(head_groups):
        query_group, key_group, value_group = head_slices(
            query_heavy, gathered_keyval, group_index, group_cols, heavy_width
        )
        scores = (
            jnp.einsum("qhd,khd->hqk", query_group, key_group, preferred_element_type=jnp.float32)
            * heavy_scale
        )
        weights, row_peak, row_guard = heavy_softmax(scores, heavy_allowed)
        heavy_parts.append(
            jnp.einsum(
                "hqk,khd->qhd",
                weights.astype(jnp.bfloat16),
                value_group,
                preferred_element_type=jnp.float32,
            ).reshape(slot_rows, group_cols)
        )
        heavy_stats.append((row_peak, row_guard))
    heavy_attended = jnp.concatenate(heavy_parts, 1)
    heavy_rescaled = (score_query[:, None] * heavy_attended).astype(jnp.bfloat16)
    residual = residual + scatter_rows(chosen[0], matmul(heavy_rescaled, heavy_output_weight))
    normed_feed = rms_norm(residual, feedforward_gain)
    feedforward_lower = normed_feed.astype(jnp.bfloat16)
    pair_light = matmul(feedforward_lower, light_expand)
    gated_light = gated_gelu(pair_light).astype(jnp.bfloat16)
    feedforward_router_scores = jax.nn.sigmoid(
        pick_values(chosen[2], jnp.dot(normed_feed, router[2], precision=HIGHEST))
    )
    feedforward_row_index = matmul(chosen_low[2], feedforward_lower).astype(jnp.bfloat16)
    pair_heavy = matmul(feedforward_row_index, heavy_expand)
    gated_heavy = gated_gelu(pair_heavy).astype(jnp.bfloat16)
    unnormed_feedforward = matmul(gated_heavy, heavy_reduce)
    output = (
        residual
        + matmul(gated_light, light_reduce)
        + scatter_rows(chosen[2], feedforward_router_scores[:, None] * unnormed_feedforward)
    ).astype(jnp.bfloat16)
    grad_gated_light = matmul_right(cotangent, light_reduce)
    grad_light_reduce = matmul_left(gated_light, cotangent)
    grad_pair_light = jax.vjp(gated_gelu, pair_light)[1](grad_gated_light)[0].astype(jnp.bfloat16)
    grad_light_expand = matmul_left(feedforward_lower, grad_pair_light)
    grad_feed = matmul_right(grad_pair_light, light_expand)
    grad_feed_rows = matmul(chosen_low[2], cotangent)
    grad_score_feed = jnp.sum(grad_feed_rows * unnormed_feedforward, 1)
    grad_raw_feed = (feedforward_router_scores[:, None] * grad_feed_rows).astype(jnp.bfloat16)
    grad_heavy_reduce = matmul_left(gated_heavy, grad_raw_feed)
    grad_gated_heavy = matmul_right(grad_raw_feed, heavy_reduce)
    grad_pair_heavy = jax.vjp(gated_gelu, pair_heavy)[1](grad_gated_heavy)[0].astype(jnp.bfloat16)
    grad_heavy_expand = matmul_left(feedforward_row_index, grad_pair_heavy)
    grad_feed = grad_feed + scatter_rows(chosen[2], matmul_right(grad_pair_heavy, heavy_expand))
    token_logit_feed = pick_back(
        chosen[2], grad_score_feed * feedforward_router_scores * (1.0 - feedforward_router_scores)
    )
    grad_feed = grad_feed + token_logit_feed[:, None] * router[2][None, :]
    router_feed = jnp.dot(token_logit_feed, normed_feed, precision=HIGHEST)
    grad_residual_norm, grad_feed_gain = jax.vjp(rms_norm, residual, feedforward_gain)[1](grad_feed)
    grad_residual = cotangent.astype(jnp.float32) + grad_residual_norm
    grad_residual_low = grad_residual.astype(jnp.bfloat16)
    grad_light_output = matmul_left(attended, grad_residual_low)
    grad_attended = matmul_right(grad_residual_low, light_output).astype(jnp.bfloat16)
    grad_heavy_rows = matmul(chosen_low[0], grad_residual_low).astype(jnp.bfloat16)
    grad_heavy_output = matmul_left(heavy_rescaled, grad_heavy_rows)
    grad_scaled = matmul_right(grad_heavy_rows, heavy_output_weight)
    grad_score_query = jnp.sum(grad_scaled * heavy_attended, 1)
    grad_heavy_attended = (score_query[:, None] * grad_scaled).astype(jnp.bfloat16)
    query_parts = []
    inner_parts = []
    for group_index in range(head_groups):
        query_group, key_group, value_group = head_slices(
            query_heavy, gathered_keyval, group_index, group_cols, heavy_width
        )
        row_peak, row_guard = heavy_stats[group_index]
        scores = (
            jnp.einsum("qhd,khd->hqk", query_group, key_group, preferred_element_type=jnp.float32)
            * heavy_scale
        )
        weights = heavy_weights(scores, heavy_allowed, row_peak, row_guard)
        grad_group = grad_heavy_attended[
            :, group_index * group_cols : (group_index + 1) * group_cols
        ].reshape(slot_rows, heads_here, HHS)
        grad_scores, inner = softmax_back(weights, grad_group, value_group)
        query_parts.append(
            (
                jnp.einsum(
                    "hqk,khd->qhd", grad_scores, key_group, preferred_element_type=jnp.float32
                )
                * heavy_scale
            ).reshape(slot_rows, group_cols)
        )
        inner_parts.append(inner)
    own_peaks = [stat[0] for stat in heavy_stats]
    own_guards = [stat[1] for stat in heavy_stats]
    key_grads = lax.psum_scatter(
        key_side(
            query_heavy,
            grad_heavy_attended,
            own_peaks,
            own_guards,
            inner_parts,
            query_segment,
            gathered_keyval,
            gathered_places,
            bounds,
            head_groups,
            group_cols,
            heavy_width,
            heavy_scale,
        ),
        "seq",
        scatter_dimension=0,
        tiled=True,
    )
    grad_keys = key_grads[:, :heavy_width].astype(jnp.bfloat16)
    grad_values = key_grads[:, heavy_width:].astype(jnp.bfloat16)
    grad_score_keyval = jnp.sum(grad_values.astype(jnp.float32) * raw_keyval[:, heavy_width:], 1)
    grad_raw_keyval = jnp.concatenate(
        [grad_keys, (score_keyval[:, None] * grad_values.astype(jnp.float32)).astype(jnp.bfloat16)],
        1,
    )
    grad_heavy_keyval = matmul_left(keyvalue_row_index, grad_raw_keyval)
    grad_query_heavy = jnp.concatenate(query_parts, 1).astype(jnp.bfloat16)
    grad_heavy_query = matmul_left(query_row_index, grad_query_heavy)
    grad_mixer = scatter_rows(
        chosen[0], matmul_right(grad_query_heavy, heavy_query)
    ) + scatter_rows(chosen[1], matmul_right(grad_raw_keyval, heavy_keyval))
    grad_padded = jnp.zeros((tok_rows + 2 * WINDOW, 2 * model_width), jnp.float32)
    light_query_parts = []
    for block_index, offset in enumerate(range(0, tok_rows, rows_block)):
        scores, allowed, query_part, key_part, value_part = light_scores(
            query_light, padded, offset, rows_block, leading_position, length, bounds
        )
        row_peak, row_total = light_stats[block_index]
        weights = jnp.exp(jnp.where(allowed[None], scores, MASKED) - row_peak) / row_total
        grad_part = grad_attended.reshape(rows_block, LH, light_size)
        grad_scores, inner = softmax_back(weights, grad_part, value_part)
        light_query_parts.append(
            (
                jnp.einsum(
                    "hqk,khd->qhd", grad_scores, key_part, preferred_element_type=jnp.float32
                )
                * light_size ** (-0.5)
            ).reshape(rows_block, model_width)
        )
        key_grad = (
            jnp.einsum("hqk,qhd->khd", grad_scores, query_part, preferred_element_type=jnp.float32)
            * light_size ** (-0.5)
        ).reshape(window_span, model_width)
        value_grad = jnp.einsum(
            "hqk,qhd->khd",
            weights.astype(jnp.bfloat16),
            grad_part,
            preferred_element_type=jnp.float32,
        ).reshape(window_span, model_width)
        grad_padded = grad_padded.at[offset : offset + window_span].add(
            jnp.concatenate([key_grad, value_grad], 1)
        )
    from_above = from_behind(grad_padded[:WINDOW].astype(jnp.bfloat16), "seq", -1).astype(
        jnp.float32
    )
    from_below = from_behind(
        grad_padded[tok_rows + WINDOW :].astype(jnp.bfloat16), "seq", 1
    ).astype(jnp.float32)
    grad_keyval_light = grad_padded[WINDOW : WINDOW + tok_rows]
    grad_keyval_light = (
        grad_keyval_light.at[:WINDOW].add(from_below).at[tok_rows - WINDOW :].add(from_above)
    )
    grad_keyval_low = grad_keyval_light.astype(jnp.bfloat16)
    grad_query_low = light_query_parts[0].astype(jnp.bfloat16)
    grad_light_query = matmul_left(attention_lower, grad_query_low)
    grad_light_keyval = matmul_left(attention_lower, grad_keyval_low)
    grad_mixer = (
        grad_mixer
        + matmul_right(grad_query_low, light_query)
        + matmul_right(grad_keyval_low, light_keyval)
    )
    token_logit_query = pick_back(chosen[0], grad_score_query * score_query * (1.0 - score_query))
    token_logit_keyval = pick_back(
        chosen[1], grad_score_keyval * score_keyval * (1.0 - score_keyval)
    )
    grad_mixer = (
        grad_mixer
        + token_logit_query[:, None] * router[0][None, :]
        + token_logit_keyval[:, None] * router[1][None, :]
    )
    grad_router = jnp.stack(
        [
            jnp.dot(token_logit_query, normed_mixer, precision=HIGHEST),
            jnp.dot(token_logit_keyval, normed_mixer, precision=HIGHEST),
            router_feed,
        ]
    )
    grad_inputs_norm, grad_attention_gain = jax.vjp(rms_norm, inputs, attention_gain)[1](grad_mixer)
    grad_tokens = (grad_residual + grad_inputs_norm).astype(jnp.bfloat16)
    row_parts = (
        lax.psum_scatter(grad_attention_gain, "seq", scatter_dimension=0, tiled=True),
        lax.psum_scatter(grad_feed_gain, "seq", scatter_dimension=0, tiled=True),
        lax.psum_scatter(grad_router, "seq", scatter_dimension=1, tiled=True),
        lax.psum_scatter(grad_light_query, "seq", scatter_dimension=0, tiled=True),
        lax.psum_scatter(grad_light_keyval, "seq", scatter_dimension=0, tiled=True),
        lax.psum_scatter(grad_light_output, "seq", scatter_dimension=0, tiled=True),
        lax.psum_scatter(grad_heavy_query, "seq", scatter_dimension=0, tiled=True),
        lax.psum_scatter(grad_heavy_keyval, "seq", scatter_dimension=0, tiled=True),
        lax.psum_scatter(grad_heavy_output, "seq", scatter_dimension=0, tiled=True),
        lax.psum_scatter(grad_light_expand, "seq", scatter_dimension=0, tiled=True),
        lax.psum_scatter(grad_light_reduce, "seq", scatter_dimension=0, tiled=True),
        lax.psum_scatter(grad_heavy_expand, "seq", scatter_dimension=0, tiled=True),
        lax.psum_scatter(grad_heavy_reduce, "seq", scatter_dimension=0, tiled=True),
    )
    matrices = (
        lax.psum_scatter(
            row_parts[3].astype(jnp.bfloat16), "dp", scatter_dimension=1, tiled=True
        ).astype(jnp.float32),
        lax.psum_scatter(
            row_parts[4].astype(jnp.bfloat16), "dp", scatter_dimension=1, tiled=True
        ).astype(jnp.float32),
        lax.psum_scatter(
            row_parts[5].astype(jnp.bfloat16), "dp", scatter_dimension=1, tiled=True
        ).astype(jnp.float32),
        lax.psum_scatter(
            row_parts[6].astype(jnp.bfloat16), "dp", scatter_dimension=1, tiled=True
        ).astype(jnp.float32),
        lax.psum_scatter(
            row_parts[7].astype(jnp.bfloat16), "dp", scatter_dimension=1, tiled=True
        ).astype(jnp.float32),
        lax.psum_scatter(
            row_parts[8].astype(jnp.bfloat16), "dp", scatter_dimension=1, tiled=True
        ).astype(jnp.float32),
        lax.psum_scatter(
            row_parts[9].astype(jnp.bfloat16), "dp", scatter_dimension=1, tiled=True
        ).astype(jnp.float32),
        lax.psum_scatter(
            row_parts[10].astype(jnp.bfloat16), "dp", scatter_dimension=1, tiled=True
        ).astype(jnp.float32),
        lax.psum_scatter(
            row_parts[11].astype(jnp.bfloat16), "dp", scatter_dimension=1, tiled=True
        ).astype(jnp.float32),
        lax.psum_scatter(
            row_parts[12].astype(jnp.bfloat16), "dp", scatter_dimension=1, tiled=True
        ).astype(jnp.float32),
    )
    small_sums = lax.psum((row_parts[0], row_parts[1], row_parts[2]), "dp")
    return (
        output,
        grad_tokens,
        small_sums[0],
        small_sums[1],
        small_sums[2],
        matrices[0],
        matrices[1],
        matrices[2],
        matrices[3],
        matrices[4],
        matrices[5],
        matrices[6],
        matrices[7],
        matrices[8],
        matrices[9],
    )


def solution(mesh):
    placed = (
        P(("dp", "seq"), None),
        P(("dp", "seq"), None),
        P(),
        P(None, ("dp", "seq")),
        P(),
        P(),
        P(),
        P(),
        P(),
        P(),
        P(),
        P(),
        P(),
        P(),
        P(),
        P(),
        P(),
    )
    return jax.shard_map(
        on_device,
        mesh=mesh,
        in_specs=placed,
        out_specs=(
            P(("dp", "seq"), None),
            P(("dp", "seq"), None),
            P("seq"),
            P("seq"),
            P(None, "seq"),
            P("seq", "dp"),
            P("seq", "dp"),
            P("seq", "dp"),
            P("seq", "dp"),
            P("seq", "dp"),
            P("seq", "dp"),
            P("seq", "dp"),
            P("seq", "dp"),
            P("seq", "dp"),
            P("seq", "dp"),
        ),
        check_vma=False,
    )
```

profile of v0, /device:TPU:0, one launch (start us, length us, event | category | flops | bytes accessed | tf_op | source)
XLA Modules:
  0.0 1907.7 jit_solution(11932628851106488524)
XLA Ops:
  30.4 24.6 %all-reduce.4 = s32[512]{0:T(512)S(1)} all-reduce(s32[512]{0:T(512)S(1)} %bitcast_dynamic-update-slice_fusion), channel_id=2, replica_groups=mesh['dp'=4,'seq'=8] {'seq'}, use_global_device_ids=true, to_apply=%add.4 | all-reduce | flops 512 | bytes 4096
  81.9 10.9 fusion.174
  92.8 7.2 fusion.40
  139.3 7.5 fusion.182
  155.0 9.3 fusion.96
  231.7 11.1 multiply_reduce_fusion
  271.6 18.4 collective-permute-done.2
  296.8 6.7 fusion.90
  309.1 6.5 fusion.153
  317.1 10.4 fusion.95
  327.6 43.1 %reduce-scatter.47.cloned.1.call-done = f32[96,768]{1,0:T(8,128)} async-done(((f32[768,768]{1,0:T(8,128)}), f32[96,768]{1,0:T(8,128)}) %reduce-scatter.47.cloned.1.call-update) | async-done | bytes 294928 | tf_op jit(solution)/shard_map/reduce_scatter | solution.py:481
  372.6 69.7 %reduce-scatter.53.cloned.1.call-done = f32[96,768]{1,0:T(8,128)} async-done(((f32[768,768]{1,0:T(8,128)}), f32[96,768]{1,0:T(8,128)}) %reduce-scatter.53.cloned.1.call-update) | async-done | bytes 294928 | tf_op jit(solution)/shard_map/reduce_scatter | solution.py:484
  444.1 69.7 %reduce-scatter.49.cloned.1.call-done = f32[96,768]{1,0:T(8,128)} async-done(((f32[768,768]{1,0:T(8,128)}), f32[96,768]{1,0:T(8,128)}) %reduce-scatter.49.cloned.1.call-update) | async-done | bytes 294928 | tf_op jit(solution)/shard_map/reduce_scatter | solution.py:482
  516.8 68.4 %reduce-scatter.43.cloned.1.call-done = f32[96,768]{1,0:T(8,128)} async-done(((f32[768,768]{1,0:T(8,128)}), f32[96,768]{1,0:T(8,128)}) %reduce-scatter.43.cloned.1.call-update) | async-done | bytes 294928 | tf_op jit(solution)/shard_map/reduce_scatter | solution.py:479
  590.4 71.7 %reduce-scatter.59.cloned.1.call-done = f32[128,768]{1,0:T(8,128)} async-done(((f32[1024,768]{1,0:T(8,128)}), f32[128,768]{1,0:T(8,128)}) %reduce-scatter.59.cloned.1.call-update) | async-done | bytes 393232 | tf_op jit(solution)/shard_map/reduce_scatter | solution.py:486
  664.0 96.1 %reduce-scatter.45.cloned.1.call-done = f32[96,1536]{1,0:T(8,128)} async-done(((f32[768,1536]{1,0:T(8,128)}), f32[96,1536]{1,0:T(8,128)}) %reduce-scatter.45.cloned.1.call-update) | async-done | bytes 589840 | tf_op jit(solution)/shard_map/reduce_scatter | solution.py:480
  762.3 119.2 %reduce-scatter.55.cloned.1.call-done = f32[96,2048]{1,0:T(8,128)} async-done(((f32[768,2048]{1,0:T(8,128)}), f32[96,2048]{1,0:T(8,128)}) %reduce-scatter.55.cloned.1.call-update) | async-done | bytes 786448 | tf_op jit(solution)/shard_map/reduce_scatter | solution.py:485
  883.5 95.9 %reduce-scatter.51.cloned.1.call-done = f32[96,1536]{1,0:T(8,128)} async-done(((f32[768,1536]{1,0:T(8,128)}), f32[96,1536]{1,0:T(8,128)}) %reduce-scatter.51.cloned.1.call-update) | async-done | bytes 589840 | tf_op jit(solution)/shard_map/reduce_scatter | solution.py:483
  981.5 208.6 %reduce-scatter.65.cloned.1.call-done = f32[512,768]{1,0:T(8,128)} async-done(((f32[4096,768]{1,0:T(8,128)}), f32[512,768]{1,0:T(8,128)}) %reduce-scatter.65.cloned.1.call-update) | async-done | bytes 1572880 | tf_op jit(solution)/shard_map/reduce_scatter | solution.py:488
  1193.8 403.0 %reduce-scatter.61.cloned.1.call-done = f32[96,8192]{1,0:T(8,128)} async-done(((f32[768,8192]{1,0:T(8,128)}), f32[96,8192]{1,0:T(8,128)}) %reduce-scatter.61.cloned.1.call-update) | async-done | bytes 3145744 | tf_op jit(solution)/shard_map/reduce_scatter | solution.py:487
  1609.5 9.1 reduce-scatter.73.cloned.1.call-done
  1620.2 20.5 %reduce-scatter.79.cloned.1.call-done = bf16[192,96]{1,0:T(8,128)(2,1)} async-done(((bf16[768,96]{1,0:T(8,128)(2,1)}), bf16[192,96]{1,0:T(8,128)(2,1)}) %reduce-scatter.79.cloned.1.call-update) | async-done | bytes 36880
  1642.2 20.5 %reduce-scatter.75.cloned.1.call-done = bf16[192,96]{1,0:T(8,128)(2,1)} async-done(((bf16[768,96]{1,0:T(8,128)(2,1)}), bf16[192,96]{1,0:T(8,128)(2,1)}) %reduce-scatter.75.cloned.1.call-update) | async-done | bytes 36880
  1664.3 21.1 %reduce-scatter.69.cloned.1.call-done = bf16[192,96]{1,0:T(8,128)(2,1)} async-done(((bf16[768,96]{1,0:T(8,128)(2,1)}), bf16[192,96]{1,0:T(8,128)(2,1)}) %reduce-scatter.69.cloned.1.call-update) | async-done | bytes 36880
  1696.4 21.7 %all-reduce.7 = (f32[768]{0:T(1024)S(1)}, f32[768]{0:T(1024)S(1)}) all-reduce(f32[768]{0:T(1024)S(1)} %get-tuple-element.121, f32[768]{0:T(1024)S(1)} %copy-done.87), channel_id=4, replica_groups=mesh['dp'=4,'seq'=8] {'seq'}, use_global_device_ids=true, to_apply=%region_27.28.clone | all-reduce | flops 1536 | bytes 12288
  1721.1 29.3 %reduce-scatter.67.cloned.1.call-done = f32[96,3]{1,0:T(8,128)} async-done(((f32[768,3]{1,0:T(8,128)}), f32[96,3]{1,0:T(8,128)}) %reduce-scatter.67.cloned.1.call-update) | async-done | bytes 1168
  1757.5 14.0 reduce-scatter.81.cloned.1.call-done
  1773.2 21.7 %reduce-scatter.71.cloned.1.call-done = bf16[384,96]{1,0:T(8,128)(2,1)} async-done(((bf16[1536,96]{1,0:T(8,128)(2,1)}), bf16[384,96]{1,0:T(8,128)(2,1)}) %reduce-scatter.71.cloned.1.call-update) | async-done | bytes 73744
  1796.7 21.4 %reduce-scatter.57.cloned.1.call-done = bf16[96,512]{1,0:T(8,128)(2,1)} async-done(((bf16[96,2048]{1,0:T(8,128)(2,1)}), bf16[96,512]{1,0:T(8,128)(2,1)}) %reduce-scatter.57.cloned.1.call-update) | async-done | bytes 98320 | tf_op jit(solution)/shard_map/reduce_scatter | solution.py:509
  1819.6 21.8 %reduce-scatter.77.cloned.1.call-done = bf16[384,96]{1,0:T(8,128)(2,1)} async-done(((bf16[1536,96]{1,0:T(8,128)(2,1)}), bf16[384,96]{1,0:T(8,128)(2,1)}) %reduce-scatter.77.cloned.1.call-update) | async-done | bytes 73744
  1843.1 24.7 %reduce-scatter.83.cloned.1.call-done = bf16[192,512]{1,0:T(8,128)(2,1)} async-done(((bf16[768,512]{1,0:T(8,128)(2,1)}), bf16[192,512]{1,0:T(8,128)(2,1)}) %reduce-scatter.83.cloned.1.call-update) | async-done | bytes 196624
  1869.7 29.0 %reduce-scatter.63.cloned.1.call-done = bf16[96,2048]{1,0:T(8,128)(2,1)} async-done(((bf16[96,8192]{1,0:T(8,128)(2,1)}), bf16[96,2048]{1,0:T(8,128)(2,1)}) %reduce-scatter.63.cloned.1.call-update) | async-done | bytes 393232 | tf_op jit(solution)/shard_map/reduce_scatter | solution.py:515
  (483 shorter events, 277.5 us)
Async XLA Ops:
  7.2 141.8 %copy-start = (bf16[768,2048]{1,0:T(8,128)(2,1)S(1)}, bf16[768,2048]{1,0:T(8,128)(2,1)}, u32[]{:S(2)}) copy-start(bf16[768,2048]{1,0:T(8,128)(2,1)} %param.38) | copy-start | bytes 9437188
  7.2 95.6 %all-gather.3.cloned.1.call-start = ((), (), s32[]{:S(2)}) async-start(), calls=%async_computation.22 | async-start | bytes 1769472 | tf_op jit(solution)/shard_map/all_gather | solution.py:273
  16.0 287.7 %reduce-scatter.41.cloned.1.call-start = ((), (), s32[]{:S(2)}) async-start(), calls=%async_computation.23 | async-start | bytes 3538944 | tf_op jit(solution)/shard_map/reduce_scatter | solution.py:374
  21.5 52.2 %collective-permute-start = (bf16[128,1536]{1,0:T(8,128)(2,1)}, bf16[128,1536]{1,0:T(8,128)(2,1)}, u32[]{:S(2)}, u32[]{:S(2)}) collective-permute-start(bf16[128,1536]{1,0:T(8,128)(2,1)} %get-tuple-element.152), channel_id=1, source_target_pairs={{0,1},{1,2},{2,3},{3,4},{4,5},{5,6},{6,7},{8,9},{9,10},{10,11},{11... | collective-permute-start | bytes 1179656 | tf_op jit(solution)/shard_map/ppermute | solution.py:24
  27.1 46.6 %collective-permute-start.1 = (bf16[128,1536]{1,0:T(8,128)(2,1)}, bf16[128,1536]{1,0:T(8,128)(2,1)}, u32[]{:S(2)}, u32[]{:S(2)}) collective-permute-start(bf16[128,1536]{1,0:T(8,128)(2,1)} %get-tuple-element.153), channel_id=1, source_target_pairs={{1,0},{2,1},{3,2},{4,3},{5,4},{6,5},{7,6},{9,8},{10,9},{11,10},{12... | collective-permute-start | bytes 1179656 | tf_op jit(solution)/shard_map/ppermute | solution.py:26
  218.0 152.7 %reduce-scatter.47.cloned.1.call-start = ((), (), s32[]{:S(2)}) async-start(), calls=%async_computation.26 | async-start | bytes 2654208 | tf_op jit(solution)/shard_map/reduce_scatter | solution.py:481
  221.4 220.9 %reduce-scatter.53.cloned.1.call-start = ((), (), s32[]{:S(2)}) async-start(), calls=%async_computation.29 | async-start | bytes 2654208 | tf_op jit(solution)/shard_map/reduce_scatter | solution.py:484
  224.4 289.4 %reduce-scatter.49.cloned.1.call-start = ((), (), s32[]{:S(2)}) async-start(), calls=%async_computation.27 | async-start | bytes 2654208 | tf_op jit(solution)/shard_map/reduce_scatter | solution.py:482
  228.2 357.0 %reduce-scatter.43.cloned.1.call-start = ((), (), s32[]{:S(2)}) async-start(), calls=%async_computation.24 | async-start | bytes 2654208 | tf_op jit(solution)/shard_map/reduce_scatter | solution.py:479
  254.1 407.9 %reduce-scatter.59.cloned.1.call-start = ((), (), s32[]{:S(2)}) async-start(), calls=%async_computation.32 | async-start | bytes 3538944 | tf_op jit(solution)/shard_map/reduce_scatter | solution.py:486
  258.3 501.9 %reduce-scatter.45.cloned.1.call-start = ((), (), s32[]{:S(2)}) async-start(), calls=%async_computation.25 | async-start | bytes 5308416 | tf_op jit(solution)/shard_map/reduce_scatter | solution.py:480
  268.5 21.5 %collective-permute-start.2 = (bf16[128,1536]{0,1:T(8,128)(2,1)S(1)}, bf16[128,1536]{0,1:T(8,128)(2,1)S(1)}, u32[]{:S(2)}, u32[]{:S(2)}) collective-permute-start(bf16[128,1536]{0,1:T(8,128)(2,1)S(1)} %get-tuple-element.143), channel_id=1, source_target_pairs={{0,1},{1,2},{2,3},{3,4},{4,5},{5,6},{6,7},{8,9},{9,10},{10,11},{11... | collective-permute-start | bytes 1179656 | tf_op jit(solution)/shard_map/ppermute | solution.py:36
  269.8 20.3 %collective-permute-start.3 = (bf16[128,1536]{0,1:T(8,128)(2,1)S(1)}, bf16[128,1536]{0,1:T(8,128)(2,1)S(1)}, u32[]{:S(2)}, u32[]{:S(2)}) collective-permute-start(bf16[128,1536]{0,1:T(8,128)(2,1)S(1)} %get-tuple-element.142), channel_id=1, source_target_pairs={{1,0},{2,1},{3,2},{4,3},{5,4},{6,5},{7,6},{9,8},{10,9},{11,10},{12... | collective-permute-start | bytes 1179656 | tf_op jit(solution)/shard_map/ppermute | solution.py:36
  295.7 585.8 %reduce-scatter.55.cloned.1.call-start = ((), (), s32[]{:S(2)}) async-start(), calls=%async_computation.30 | async-start | bytes 7077888 | tf_op jit(solution)/shard_map/reduce_scatter | solution.py:485
  303.6 675.9 %reduce-scatter.51.cloned.1.call-start = ((), (), s32[]{:S(2)}) async-start(), calls=%async_computation.28 | async-start | bytes 5308416 | tf_op jit(solution)/shard_map/reduce_scatter | solution.py:483
  307.9 882.2 %reduce-scatter.65.cloned.1.call-start = ((), (), s32[]{:S(2)}) async-start(), calls=%async_computation.35 | async-start | bytes 14155776 | tf_op jit(solution)/shard_map/reduce_scatter | solution.py:488
  315.6 1281.2 %reduce-scatter.61.cloned.1.call-start = ((), (), s32[]{:S(2)}) async-start(), calls=%async_computation.33 | async-start | bytes 28311552 | tf_op jit(solution)/shard_map/reduce_scatter | solution.py:487
  327.5 188.2 %copy-start.94 = (f32[64]{0:T(128)S(1)}, f32[64]{0:T(128)}, u32[]{:S(2)}) copy-start(f32[64]{0:T(128)} %copy-done.91) | copy-start | bytes 772
  327.5 188.2 %copy-start.107 = (f32[64]{0:T(128)S(1)}, f32[64]{0:T(128)}, u32[]{:S(2)}) copy-start(f32[64]{0:T(128)} %get-tuple-element.156) | copy-start | bytes 772
  327.6 188.2 %copy-start.4 = (f32[512,768]{1,0:T(8,128)S(1)}, f32[512,768]{1,0:T(8,128)}, u32[]{:S(2)}) copy-start(f32[512,768]{1,0:T(8,128)} %copy-done.3) | copy-start | bytes 4718596
  327.6 188.2 %copy-start.81 = (f32[512]{0:T(512)S(1)}, f32[512]{0:T(512)}, u32[]{:S(2)}) copy-start(f32[512]{0:T(512)} %copy-done.80) | copy-start | bytes 6148
  327.6 1291.1 %reduce-scatter.73.cloned.1.call-start = ((), (), s32[]{:S(2)}) async-start(), calls=%async_computation.39 | async-start | bytes 245760
  372.5 1268.2 %reduce-scatter.79.cloned.1.call-start = ((), (), s32[]{:S(2)}) async-start(), calls=%async_computation.42 | async-start | bytes 245760
  444.1 1218.7 %reduce-scatter.75.cloned.1.call-start = ((), (), s32[]{:S(2)}) async-start(), calls=%async_computation.40 | async-start | bytes 245760
  515.6 1169.7 %reduce-scatter.69.cloned.1.call-start = ((), (), s32[]{:S(2)}) async-start(), calls=%async_computation.37 | async-start | bytes 245760
  587.0 1163.4 %reduce-scatter.67.cloned.1.call-start = ((), (), s32[]{:S(2)}) async-start(), calls=%async_computation.36 | async-start | bytes 442368
  590.3 1181.2 %reduce-scatter.81.cloned.1.call-start = ((), (), s32[]{:S(2)}) async-start(), calls=%async_computation.43 | async-start | bytes 245760
  663.9 1130.9 %reduce-scatter.71.cloned.1.call-start = ((), (), s32[]{:S(2)}) async-start(), calls=%async_computation.38 | async-start | bytes 491520
  762.2 1055.8 %reduce-scatter.57.cloned.1.call-start = ((), (), s32[]{:S(2)}) async-start(), calls=%async_computation.31 | async-start | bytes 491520 | tf_op jit(solution)/shard_map/reduce_scatter | solution.py:509
  883.4 958.0 %reduce-scatter.77.cloned.1.call-start = ((), (), s32[]{:S(2)}) async-start(), calls=%async_computation.41 | async-start | bytes 491520
  981.5 886.3 %reduce-scatter.83.cloned.1.call-start = ((), (), s32[]{:S(2)}) async-start(), calls=%async_computation.44 | async-start | bytes 983040
  1192.8 705.9 %reduce-scatter.63.cloned.1.call-start = ((), (), s32[]{:S(2)}) async-start(), calls=%async_computation.34 | async-start | bytes 1966080 | tf_op jit(solution)/shard_map/reduce_scatter | solution.py:515
  (112 other events, 913.1 us)
Sparse Core Ops, SparseCore 0:
  16.1 50.6 all-gather.2
  218.1 79.0 reduce-scatter.40
  300.7 69.9 reduce-scatter.46
  374.0 68.1 reduce-scatter.52
  445.6 68.1 reduce-scatter.48
  517.2 68.0 reduce-scatter.42
  588.8 73.2 reduce-scatter.58
  665.7 94.3 reduce-scatter.44
  763.7 117.7 reduce-scatter.54
  885.0 94.3 reduce-scatter.50
  983.0 207.0 reduce-scatter.64
  1193.9 402.8 reduce-scatter.60
  1599.8 18.8 reduce-scatter.72
  1620.9 19.7 reduce-scatter.78
  1643.0 19.7 reduce-scatter.74
  1665.6 19.7 reduce-scatter.68
  1689.1 61.3 reduce-scatter.66
  1752.7 18.7 reduce-scatter.80
  1774.0 20.7 reduce-scatter.70
  1797.2 20.7 reduce-scatter.56
  1820.5 20.8 reduce-scatter.76
  1844.5 23.2 reduce-scatter.82
  1870.5 28.1 reduce-scatter.62
where the time goes:
time: 1920 us; the launch traced here: 1910 us
  waiting for transfers between devices  1500 us (78%)
  matrix products  196 us (10%)
  local copies, waits for them, and re-layouts  83.8 us (4%)
  blocking collectives  52.6 us (3%)
  other arithmetic  49.6 us (3%)
    reduce_scatter x1, waiting for transfers between devices, on_device(): lax.psum_scatter(grad_heavy_expand, 'seq', scatter_dimension=0, tiled=True)  403 us
    reduce_scatter x1, waiting for transfers between devices, on_device(): lax.psum_scatter(grad_heavy_reduce, 'seq', scatter_dimension=0, tiled=True)  209 us
    unnamed x32, waiting for transfers between devices  183 us
    reduce_scatter x1, waiting for transfers between devices, on_device(): lax.psum_scatter(grad_light_expand, 'seq', scatter_dimension=0, tiled=True)  119 us
    reduce_scatter x1, waiting for transfers between devices, on_device(): lax.psum_scatter(grad_light_keyval, 'seq', scatter_dimension=0, tiled=True)  96.1 us
    reduce_scatter x1, waiting for transfers between devices, on_device(): lax.psum_scatter(grad_heavy_keyval, 'seq', scatter_dimension=0, tiled=True)  95.9 us
    reduce_scatter x1, waiting for transfers between devices, on_device(): lax.psum_scatter(grad_light_reduce, 'seq', scatter_dimension=0, tiled=True)  71.7 us
    reduce_scatter x1, waiting for transfers between devices, on_device(): lax.psum_scatter(grad_heavy_query, 'seq', scatter_dimension=0, tiled=True)  69.7 us
  transfers between devices with their start and end apart: 27, of which 22 were waited for; matrix products, arithmetic and copies ran while one was open for 10% of the time, Pallas kernels for 0%

commit v1 on v0

--- a/solution.py
+++ b/solution.py
@@ -144,62 +144,145 @@
     return ((weights * (grad_weights - inner)).astype(jnp.bfloat16), inner)
 
 
-def key_side(
-    query_rows,
-    grad_rows,
-    peaks,
-    guards,
-    inners,
-    query_segment,
-    key_rows,
-    key_places,
-    bounds,
-    head_groups,
-    group_cols,
-    heavy_width,
-    heavy_scale,
-):
-    row_count = key_rows.shape[0]
-    query_count = query_rows.shape[0]
-    heads_here = group_cols // HHS
-    allowed_part = (key_places[None, :] >= 0) & (
-        query_segment[:, None] == segment_of(key_places, bounds)[None, :]
-    )
-    key_parts = []
-    value_parts = []
-    for group_index in range(head_groups):
-        query_group, key_group, value_group = head_slices(
-            query_rows, key_rows, group_index, group_cols, heavy_width
-        )
-        scores = (
-            jnp.einsum("qhd,khd->hqk", query_group, key_group, preferred_element_type=jnp.float32)
-            * heavy_scale
-        )
-        weights = heavy_weights(scores, allowed_part, peaks[group_index], guards[group_index])
-        grad_group = grad_rows[
-            :, group_index * group_cols : (group_index + 1) * group_cols
-        ].reshape(query_count, heads_here, HHS)
-        grad_weights = jnp.einsum(
-            "qhd,khd->hqk", grad_group, value_group, preferred_element_type=jnp.float32
-        )
-        grad_scores = (weights * (grad_weights - inners[group_index])).astype(jnp.bfloat16)
-        key_parts.append(
-            (
-                jnp.einsum(
-                    "hqk,qhd->khd", grad_scores, query_group, preferred_element_type=jnp.float32
-                )
-                * heavy_scale
-            ).reshape(row_count, group_cols)
-        )
-        value_parts.append(
-            jnp.einsum(
-                "hqk,qhd->khd",
-                weights.astype(jnp.bfloat16),
-                grad_group,
-                preferred_element_type=jnp.float32,
-            ).reshape(row_count, group_cols)
-        )
-    return jnp.concatenate(key_parts + value_parts, 1)
+def stages(count):
+    found, stride = [], 1
+    while count > 1:
+        size = 4 if count % 4 == 0 and count != 8 else 2
+        found.append((size, stride))
+        stride, count = stride * size, count // size
+    return found
+
+
+def shifted(block, axis, size, stride, step):
+    count = lax.axis_size(axis)
+    route = []
+    for i in range(count):
+        member = (i // stride) % size
+        route.append((i, i + ((member + step) % size - member) * stride))
+    return lax.ppermute(block, axis, route)
+
+
+def member_of(axis, size, stride):
+    return (lax.axis_index(axis) // stride) % size
+
+
+def pick(block, index, dim):
+    return lax.dynamic_index_in_dim(block, index, dim, keepdims=False)
+
+
+def reduce_stage(block, axis, size, stride, dim):
+    me = member_of(axis, size, stride)
+    total = pick(block, me, dim).astype(jnp.float32)
+    for step in range(1, size):
+        sent = pick(block, (me + step) % size, dim).astype(jnp.bfloat16)
+        total = total + shifted(sent, axis, size, stride, step).astype(jnp.float32)
+    return total
+
+
+def reduce_dp(block):
+    rows, columns = block.shape[1:]
+    block = reduce_stage(block.reshape(2, 2, rows, columns), "dp", 2, 1, 1)
+    return reduce_stage(block, "dp", 2, 2, 0)
+
+
+def reduce_seq(block, skip=0):
+    for size, stride in stages(lax.axis_size("seq"))[skip:]:
+        count = lax.axis_size("seq") // stride
+        block = block.reshape(count // size, size, block.shape[0] // count, block.shape[1])
+        block = reduce_stage(block, "seq", size, stride, 1)
+        block = block.reshape(-1, block.shape[-1])
+    return block
+
+
+def gather_seq(block):
+    for size, stride in stages(lax.axis_size("seq")):
+        block = jnp.concatenate(
+            [block] + [shifted(block, "seq", size, stride, step) for step in range(1, size)], 0
+        )
+    return block
+
+
+def gather_dp(former, latter):
+    rows, columns = latter.shape
+    latter = latter.reshape(rows, 2, 2, columns // 4)
+    core, x = member_of("dp", 2, 1), member_of("dp", 2, 2)
+    mine = pick(latter, core, 2)
+    other = pick(latter, 1 - core, 2).reshape(rows, columns // 2)
+    got = shifted(jnp.concatenate([former, other], 1), "dp", 2, 1, 1)
+    width = former.shape[1]
+    former = jnp.concatenate([former, got[:, :width]], 0)
+    latter = jnp.concatenate([mine, got[:, width:].reshape(rows, 2, columns // 4)], 0)
+    mine, other = pick(latter, x, 1), pick(latter, 1 - x, 1)
+    got = shifted(jnp.concatenate([former, other], 1), "dp", 2, 2, 1)
+    former = jnp.concatenate([former, got[:, :width]], 0)
+    latter = jnp.concatenate([mine, got[:, width:]], 0)
+    return former, latter
+
+
+def quarters(former, latter):
+    parts = latter.reshape(latter.shape[0], 4, latter.shape[1] // 4)
+    return jnp.stack([matmul_left(former, parts[:, i]) for i in range(4)]).astype(jnp.bfloat16)
+
+
+def light_gradient(former, latter):
+    return reduce_seq(reduce_dp(quarters(former, latter)))
+
+
+def heavy_gradient(former, latter):
+    former, latter = gather_dp(former, latter)
+    return reduce_seq(matmul_left(former, latter))
+
+
+def expand_gradient(former, latter):
+    former, latter = gather_dp(former, latter)
+    rows, width = former.shape
+    size, stride = stages(lax.axis_size("seq"))[0]
+    count = lax.axis_size("seq")
+    former = former.reshape(rows, count // size, size, width // count)
+    me = member_of("seq", size, stride)
+    formers, latters = [pick(former, me, 2).reshape(rows, width // size)], [latter]
+    for step in range(1, size):
+        other = pick(former, (me + step) % size, 2).reshape(rows, width // size)
+        got = shifted(jnp.concatenate([other, latter], 1), "seq", size, stride, step)
+        formers.append(got[:, : width // size])
+        latters.append(got[:, width // size :])
+    product = matmul_left(jnp.concatenate(formers, 0), jnp.concatenate(latters, 0))
+    return reduce_seq(product, 1)
+
+
+def reduce_gradient(former, latter):
+    for size, stride in stages(lax.axis_size("seq")):
+        rows, width = former.shape
+        count = lax.axis_size("seq") // stride
+        former = former.reshape(rows, count // size, size, width // count)
+        me = member_of("seq", size, stride)
+        formers, latters = [pick(former, me, 2).reshape(rows, width // size)], [latter]
+        for step in range(1, size):
+            other = pick(former, (me + step) % size, 2).reshape(rows, width // size)
+            got = shifted(jnp.concatenate([other, latter], 1), "seq", size, stride, step)
+            formers.append(got[:, : width // size])
+            latters.append(got[:, width // size :])
+        former, latter = jnp.concatenate(formers, 0), jnp.concatenate(latters, 0)
+    return reduce_dp(quarters(former, latter))
+
+
+def reduce_small(block):
+    for stride in (1, 2):
+        block = block + shifted(block, "dp", 2, stride, 1)
+    for size, stride in stages(lax.axis_size("seq")):
+        count = lax.axis_size("seq") // stride
+        block = block.reshape(block.shape[0], count // size, size, block.shape[1] // count)
+        me = member_of("seq", size, stride)
+        total = pick(block, me, 2)
+        for step in range(1, size):
+            total = total + shifted(pick(block, (me + step) % size, 2), "seq", size, stride, step)
+        block = total.reshape(total.shape[0], -1)
+    return block
+
+
+def high_low(values):
+    high = lax.reduce_precision(values, 8, 7)
+    return high.astype(jnp.bfloat16), (values - high).astype(jnp.bfloat16)
 
 
 def on_device(
@@ -269,14 +352,13 @@
         [raw_keyval[:, :heavy_width], score_keyval[:, None] * raw_keyval[:, heavy_width:]], 1
     ).astype(jnp.bfloat16)
     slot_token_positions = jnp.where(alive_flags, leading_position + routes, -1)
-    gathered_keyval, gathered_places = (
-        lax.all_gather(keyval_heavy, "seq", axis=0, tiled=True),
-        lax.all_gather(slot_token_positions[1], "seq", axis=0, tiled=True),
-    )
+    key_segment = jnp.where(alive_flags[1], segment_of(slot_token_positions[1], bounds), -1)
+    tag = jnp.pad(key_segment[:, None].astype(jnp.bfloat16), ((0, 0), (0, 127)))
+    gathered = gather_seq(jnp.concatenate([keyval_heavy, tag], 1))
+    gathered_keyval = gathered[:, : 2 * heavy_width]
+    gathered_segment = gathered[:, 2 * heavy_width].astype(jnp.int32)
     query_segment = segment_of(slot_token_positions[0], bounds)
-    heavy_allowed = (gathered_places[None, :] >= 0) & (
-        query_segment[:, None] == segment_of(gathered_places, bounds)[None, :]
-    )
+    heavy_allowed = query_segment[:, None] == gathered_segment[None, :]
     heavy_parts = []
     heavy_stats = []
     for group_index in range(head_groups):
@@ -317,17 +399,17 @@
         + scatter_rows(chosen[2], feedforward_router_scores[:, None] * unnormed_feedforward)
     ).astype(jnp.bfloat16)
     grad_gated_light = matmul_right(cotangent, light_reduce)
-    grad_light_reduce = matmul_left(gated_light, cotangent)
+    grad_light_reduce = light_gradient(gated_light, cotangent)
     grad_pair_light = jax.vjp(gated_gelu, pair_light)[1](grad_gated_light)[0].astype(jnp.bfloat16)
-    grad_light_expand = matmul_left(feedforward_lower, grad_pair_light)
+    grad_light_expand = light_gradient(feedforward_lower, grad_pair_light)
     grad_feed = matmul_right(grad_pair_light, light_expand)
     grad_feed_rows = matmul(chosen_low[2], cotangent)
     grad_score_feed = jnp.sum(grad_feed_rows * unnormed_feedforward, 1)
     grad_raw_feed = (feedforward_router_scores[:, None] * grad_feed_rows).astype(jnp.bfloat16)
-    grad_heavy_reduce = matmul_left(gated_heavy, grad_raw_feed)
+    grad_heavy_reduce = reduce_gradient(gated_heavy, grad_raw_feed)
     grad_gated_heavy = matmul_right(grad_raw_feed, heavy_reduce)
     grad_pair_heavy = jax.vjp(gated_gelu, pair_heavy)[1](grad_gated_heavy)[0].astype(jnp.bfloat16)
-    grad_heavy_expand = matmul_left(feedforward_row_index, grad_pair_heavy)
+    grad_heavy_expand = expand_gradient(feedforward_row_index, grad_pair_heavy)
     grad_feed = grad_feed + scatter_rows(chosen[2], matmul_right(grad_pair_heavy, heavy_expand))
     token_logit_feed = pick_back(
         chosen[2], grad_score_feed * feedforward_router_scores * (1.0 - feedforward_router_scores)
@@ -337,10 +419,10 @@
     grad_residual_norm, grad_feed_gain = jax.vjp(rms_norm, residual, feedforward_gain)[1](grad_feed)
     grad_residual = cotangent.astype(jnp.float32) + grad_residual_norm
     grad_residual_low = grad_residual.astype(jnp.bfloat16)
-    grad_light_output = matmul_left(attended, grad_residual_low)
+    grad_light_output = light_gradient(attended, grad_residual_low)
     grad_attended = matmul_right(grad_residual_low, light_output).astype(jnp.bfloat16)
     grad_heavy_rows = matmul(chosen_low[0], grad_residual_low).astype(jnp.bfloat16)
-    grad_heavy_output = matmul_left(heavy_rescaled, grad_heavy_rows)
+    grad_heavy_output = heavy_gradient(heavy_rescaled, grad_heavy_rows)
     grad_scaled = matmul_right(grad_heavy_rows, heavy_output_weight)
     grad_score_query = jnp.sum(grad_scaled * heavy_attended, 1)
     grad_heavy_attended = (score_query[:, None] * grad_scaled).astype(jnp.bfloat16)
@@ -369,27 +451,63 @@
             ).reshape(slot_rows, group_cols)
         )
         inner_parts.append(inner)
-    own_peaks = [stat[0] for stat in heavy_stats]
-    own_guards = [stat[1] for stat in heavy_stats]
-    key_grads = lax.psum_scatter(
-        key_side(
+    stats = []
+    for group_index in range(head_groups):
+        row_peak, row_guard = heavy_stats[group_index]
+        stats.append((row_peak + jnp.log(row_guard))[:, :, 0].T)
+    for group_index in range(head_groups):
+        stats.append(inner_parts[group_index][:, :, 0].T)
+    stat_high, stat_low = high_low(jnp.concatenate(stats, 1))
+    heads = heavy_width // HHS
+    packet = jnp.concatenate(
+        [
             query_heavy,
             grad_heavy_attended,
-            own_peaks,
-            own_guards,
-            inner_parts,
-            query_segment,
-            gathered_keyval,
-            gathered_places,
-            bounds,
-            head_groups,
-            group_cols,
-            heavy_width,
-            heavy_scale,
-        ),
-        "seq",
-        scatter_dimension=0,
-        tiled=True,
+            stat_high,
+            stat_low,
+            query_segment[:, None].astype(jnp.bfloat16),
+            jnp.zeros((slot_rows, 127 - 4 * heads), jnp.bfloat16),
+        ],
+        1,
+    )
+    packet = gather_seq(packet)
+    every_query = packet[:, :heavy_width].reshape(-1, heads, HHS)
+    every_grad = packet[:, heavy_width : 2 * heavy_width].reshape(-1, heads, HHS)
+    column = 2 * heavy_width
+    every_stat = packet[:, column : column + 2 * heads].astype(jnp.float32) + packet[
+        :, column + 2 * heads : column + 4 * heads
+    ].astype(jnp.float32)
+    every_segment = packet[:, column + 4 * heads].astype(jnp.int32)
+    own_key = keyval_heavy[:, :heavy_width].reshape(slot_rows, heads, HHS)
+    own_value = keyval_heavy[:, heavy_width:].reshape(slot_rows, heads, HHS)
+    own_allowed = every_segment[:, None] == key_segment[None, :]
+    scores = (
+        jnp.einsum("qhd,khd->hqk", every_query, own_key, preferred_element_type=jnp.float32)
+        * heavy_scale
+    )
+    weights = jnp.where(
+        own_allowed[None], jnp.exp(jnp.where(own_allowed[None], scores - every_stat[:, :heads].T[:, :, None], 0.0)), 0.0
+    )
+    grad_weights = jnp.einsum(
+        "qhd,khd->hqk", every_grad, own_value, preferred_element_type=jnp.float32
+    )
+    grad_scores = (weights * (grad_weights - every_stat[:, heads:].T[:, :, None])).astype(jnp.bfloat16)
+    key_grads = jnp.concatenate(
+        [
+            (
+                jnp.einsum(
+                    "hqk,qhd->khd", grad_scores, every_query, preferred_element_type=jnp.float32
+                )
+                * heavy_scale
+            ).reshape(slot_rows, heavy_width),
+            jnp.einsum(
+                "hqk,qhd->khd",
+                weights.astype(jnp.bfloat16),
+                every_grad,
+                preferred_element_type=jnp.float32,
+            ).reshape(slot_rows, heavy_width),
+        ],
+        1,
     )
     grad_keys = key_grads[:, :heavy_width].astype(jnp.bfloat16)
     grad_values = key_grads[:, heavy_width:].astype(jnp.bfloat16)
@@ -398,9 +516,9 @@
         [grad_keys, (score_keyval[:, None] * grad_values.astype(jnp.float32)).astype(jnp.bfloat16)],
         1,
     )
-    grad_heavy_keyval = matmul_left(keyvalue_row_index, grad_raw_keyval)
+    grad_heavy_keyval = heavy_gradient(keyvalue_row_index, grad_raw_keyval)
     grad_query_heavy = jnp.concatenate(query_parts, 1).astype(jnp.bfloat16)
-    grad_heavy_query = matmul_left(query_row_index, grad_query_heavy)
+    grad_heavy_query = heavy_gradient(query_row_index, grad_query_heavy)
     grad_mixer = scatter_rows(
         chosen[0], matmul_right(grad_query_heavy, heavy_query)
     ) + scatter_rows(chosen[1], matmul_right(grad_raw_keyval, heavy_keyval))
@@ -447,8 +565,8 @@
     )
     grad_keyval_low = grad_keyval_light.astype(jnp.bfloat16)
     grad_query_low = light_query_parts[0].astype(jnp.bfloat16)
-    grad_light_query = matmul_left(attention_lower, grad_query_low)
-    grad_light_keyval = matmul_left(attention_lower, grad_keyval_low)
+    grad_light_query = light_gradient(attention_lower, grad_query_low)
+    grad_light_keyval = light_gradient(attention_lower, grad_keyval_low)
     grad_mixer = (
         grad_mixer
         + matmul_right(grad_query_low, light_query)
@@ -472,70 +590,25 @@
     )
     grad_inputs_norm, grad_attention_gain = jax.vjp(rms_norm, inputs, attention_gain)[1](grad_mixer)
     grad_tokens = (grad_residual + grad_inputs_norm).astype(jnp.bfloat16)
-    row_parts = (
-        lax.psum_scatter(grad_attention_gain, "seq", scatter_dimension=0, tiled=True),
-        lax.psum_scatter(grad_feed_gain, "seq", scatter_dimension=0, tiled=True),
-        lax.psum_scatter(grad_router, "seq", scatter_dimension=1, tiled=True),
-        lax.psum_scatter(grad_light_query, "seq", scatter_dimension=0, tiled=True),
-        lax.psum_scatter(grad_light_keyval, "seq", scatter_dimension=0, tiled=True),
-        lax.psum_scatter(grad_light_output, "seq", scatter_dimension=0, tiled=True),
-        lax.psum_scatter(grad_heavy_query, "seq", scatter_dimension=0, tiled=True),
-        lax.psum_scatter(grad_heavy_keyval, "seq", scatter_dimension=0, tiled=True),
-        lax.psum_scatter(grad_heavy_output, "seq", scatter_dimension=0, tiled=True),
-        lax.psum_scatter(grad_light_expand, "seq", scatter_dimension=0, tiled=True),
-        lax.psum_scatter(grad_light_reduce, "seq", scatter_dimension=0, tiled=True),
-        lax.psum_scatter(grad_heavy_expand, "seq", scatter_dimension=0, tiled=True),
-        lax.psum_scatter(grad_heavy_reduce, "seq", scatter_dimension=0, tiled=True),
-    )
-    matrices = (
-        lax.psum_scatter(
-            row_parts[3].astype(jnp.bfloat16), "dp", scatter_dimension=1, tiled=True
-        ).astype(jnp.float32),
-        lax.psum_scatter(
-            row_parts[4].astype(jnp.bfloat16), "dp", scatter_dimension=1, tiled=True
-        ).astype(jnp.float32),
-        lax.psum_scatter(
-            row_parts[5].astype(jnp.bfloat16), "dp", scatter_dimension=1, tiled=True
-        ).astype(jnp.float32),
-        lax.psum_scatter(
-            row_parts[6].astype(jnp.bfloat16), "dp", scatter_dimension=1, tiled=True
-        ).astype(jnp.float32),
-        lax.psum_scatter(
-            row_parts[7].astype(jnp.bfloat16), "dp", scatter_dimension=1, tiled=True
-        ).astype(jnp.float32),
-        lax.psum_scatter(
-            row_parts[8].astype(jnp.bfloat16), "dp", scatter_dimension=1, tiled=True
-        ).astype(jnp.float32),
-        lax.psum_scatter(
-            row_parts[9].astype(jnp.bfloat16), "dp", scatter_dimension=1, tiled=True
-        ).astype(jnp.float32),
-        lax.psum_scatter(
-            row_parts[10].astype(jnp.bfloat16), "dp", scatter_dimension=1, tiled=True
-        ).astype(jnp.float32),
-        lax.psum_scatter(
-            row_parts[11].astype(jnp.bfloat16), "dp", scatter_dimension=1, tiled=True
-        ).astype(jnp.float32),
-        lax.psum_scatter(
-            row_parts[12].astype(jnp.bfloat16), "dp", scatter_dimension=1, tiled=True
-        ).astype(jnp.float32),
-    )
-    small_sums = lax.psum((row_parts[0], row_parts[1], row_parts[2]), "dp")
+    small = reduce_small(
+        jnp.concatenate([grad_attention_gain[None], grad_feed_gain[None], grad_router], 0)
+    )
     return (
         output,
         grad_tokens,
-        small_sums[0],
-        small_sums[1],
-        small_sums[2],
-        matrices[0],
-        matrices[1],
-        matrices[2],
-        matrices[3],
-        matrices[4],
-        matrices[5],
-        matrices[6],
-        matrices[7],
-        matrices[8],
-        matrices[9],
+        small[0],
+        small[1],
+        small[2:],
+        grad_light_query,
+        grad_light_keyval,
+        grad_light_output,
+        grad_heavy_query,
+        grad_heavy_keyval,
+        grad_heavy_output,
+        grad_light_expand,
+        grad_light_reduce,
+        grad_heavy_expand,
+        grad_heavy_reduce,
     )
 
 

time: 1920 us -> 700 us (0.36)
  waiting for transfers between devices: 1500 us -> 135 us
  starting transfers between devices: 10.9 us -> 116 us
  local copies, waits for them, and re-layouts: 83.8 us -> 168 us
  blocking collectives: 52.6 us -> 0 us
  other arithmetic: 49.6 us -> 91.9 us
  matrix products: 196 us -> 174 us
    reduce_scatter x13 -> x0, waiting for transfers between devices: 1300 us -> none  [the longest x1 403 us: on_device(): lax.psum_scatter(grad_heavy_expand, 'seq', scatter_dimension=0, tiled=True)]
    unnamed x32 -> x0, waiting for transfers between devices: 183 us -> none
    ppermute x0 -> x74, waiting for transfers between devices: none -> 133 us  [shifted(): return lax.ppermute(block, axis, route)]
    ppermute x0 -> x74, starting transfers between devices: none -> 108 us  [shifted(): return lax.ppermute(block, axis, route)]
    unnamed x2 -> x0, blocking collectives: 46.3 us -> none
    slice x1 -> x27, local copies, waits for them, and re-layouts: 0.01 us -> 22.6 us  [the longest x8 6.49 us: gather_dp(): former = jnp.concatenate([former, got[:, :width]], 0)]
    dynamic_slice x0 -> x20, local copies, waits for them, and re-layouts: none -> 22.5 us  [pick(): return lax.dynamic_index_in_dim(block, index, dim, keepdims=False)]
    add x1 -> x28, other arithmetic: 0.42 us -> 22.6 us  [the longest x20 20.7 us: reduce_stage(): total = total + shifted(sent, axis, size, stride, step).astype(jnp.float32)]
  transfers between devices with their start and end apart: 27 -> 78, of which waited for: 22 -> 23; matrix products, arithmetic and copies ran while one was open for 10% -> 44% of each run, Pallas kernels for 0% -> 0%
where the time goes in v1:
time: 700 us; the launch traced here: 690 us
  matrix products  174 us (25%)
  local copies, waits for them, and re-layouts  168 us (24%)
  waiting for transfers between devices  135 us (19%)
  starting transfers between devices  116 us (17%)
  other arithmetic  91.9 us (13%)
    ppermute x74, waiting for transfers between devices, shifted(): return lax.ppermute(block, axis, route)  133 us
    ppermute x74, starting transfers between devices, shifted(): return lax.ppermute(block, axis, route)  108 us
    dot_general x10, matrix products, matmul_right(): lax.dot_general(former, latter, (((1,), (1,)), ((), ())), preferred_eleme...  36.3 us
    unnamed x494, local copies, waits for them, and re-layouts  34.9 us
    dot_general x15, matrix products, matmul(): return jnp.dot(former, latter, preferred_element_type=jnp.float32)  29.9 us
    dot_general x28, matrix products, matmul_left(): lax.dot_general(former, latter, (((0,), (0,)), ((), ())), preferred_eleme...  27.4 us
    dynamic_slice x20, local copies, waits for them, and re-layouts, pick(): return lax.dynamic_index_in_dim(block, index, dim, keepdims=False)  22.5 us
    add x20, other arithmetic, reduce_stage(): total = total + shifted(sent, axis, size, stride, step).astype(jnp.float32)  20.7 us
  transfers between devices with their start and end apart: 78, of which 23 were waited for; matrix products, arithmetic and copies ran while one was open for 44% of the time, Pallas kernels for 0%

profile of v1, /device:TPU:0, one launch (start us, length us, event | category | flops | bytes accessed | tf_op | source)
XLA Modules:
  0.0 689.8 jit_solution(13949772403423102514)
XLA Ops:
  18.5 3.4 convolution_convert_fusion
  44.6 3.3 convolution_convert_fusion.2
  56.3 4.4 collective-permute-start.3
  74.1 10.8 %fusion.279 = (f32[8,512]{1,0:T(8,128)S(1)}, f32[8,512,768]{2,1,0:T(8,128)}) fusion(pred[512,768]{1,0:T(8,128)(4,1)} %fusion.42, bf16[512,8,96]{0,2,1:T(8,128)(2,1)} %bitcast.584, bf16[768,8,96]{0,2,1:T(8,128)(2,1)} %bitcast.592), kind=kOutput, calls=%fused_computation.606 | convolution fusion | flops 616563456 | bytes 14958592 | tf_op jit(solution)/shard_map/sub | solution.py:107
  84.9 7.2 %fusion.43 = bf16[8,96,512]{2,1,0:T(8,128)(2,1)S(1)} fusion(bf16[768,8,96]{0,2,1:T(8,128)(2,1)} %bitcast.626, f32[8,512,768]{2,1,0:T(8,128)} %get-tuple-element.208, f32[8,512]{1,0:T(8,128)S(1)} %get-tuple-element.207), kind=kOutput, calls=%fused_computation.89 | convolution fusion | flops 610664448 | bytes 14565376 | tf_op jit(solution)/shard_map/hqk,khd->qhd/dot_general | solution.py:331
  134.4 3.9 fusion.110
  150.1 4.3 fusion.290
  155.8 5.1 fusion.148
  165.0 9.7 %fusion.292 = f32[64,768]{1,0:T(8,128)} fusion(bf16[64,8192]{1,0:T(8,128)(2,1)} %add_convert_fusion.1, bf16[768,8192]{1,0:T(8,128)(2,1)} %param.40), kind=kOutput, calls=%fused_computation.619 | convolution fusion | flops 805306368 | bytes 13828096 | tf_op jit(solution)/shard_map/dot_general | solution.py:65
  176.3 4.5 reshape.1076
  180.8 3.5 fusion.291
  207.3 5.5 fusion.7
  212.9 10.6 %multiply_reduce_fusion = (f32[8,512]{1,0:T(8,128)S(1)}, f32[8,512,768]{2,1,0:T(8,128)}) fusion(f32[8,512,768]{2,1,0:T(8,128)} %get-tuple-element.208, f32[8,512]{1,0:T(8,128)S(1)} %copy-done.187, bf16[512,8,96]{0,2,1:T(8,128)(2,1)S(1)} %bitcast.646, bf16[768,8,96]{0,2,1:T(8,128)(2,1)S(1)} %bitcast.627), kind=kOutput, calls=%fused_computation.2 | convolution fusion | flops 613412864 | bytes 27164672 | tf_op jit(solution)/shard_map/qhd,khd->hqk/dot_general | solution.py:140
  223.5 6.3 multiply_convert_fusion
  247.1 3.6 fusion.288
  256.6 4.9 dynamic-slice_reduce_fusion
  299.5 3.2 collective-permute-start.10
  359.8 3.5 collective-permute-start.51
  391.4 17.0 %collective-permute-done.8 = bf16[128,1664]{1,0:T(8,128)(2,1)S(1)} collective-permute-done((bf16[128,1664]{1,0:T(8,128)(2,1)S(1)}, bf16[128,1664]{1,0:T(8,128)(2,1)S(1)}, u32[]{:S(2)}, u32[]{:S(2)}) %collective-permute-start.8) | collective-permute-done | bytes 426016 | tf_op jit(solution)/shard_map/ppermute | solution.py:162
  431.8 5.6 fusion.34
  443.4 3.6 fusion.37
  455.7 9.0 %collective-permute-start.15 = (f32[5,1,96]{2,1,0:T(1,128)S(1)}, f32[5,1,96]{2,1,0:T(1,128)S(1)}, u32[]{:S(2)}, u32[]{:S(2)}) collective-permute-start(f32[5,1,96]{2,1,0:T(1,128)S(1)} %get-tuple-element.198), channel_id=1, source_target_pairs={{0,2},{1,3},{2,4},{3,5},{4,6},{5,7},{6,0},{7,1},{8,10},{9,11},{10,... | collective-permute-start | bytes 5768 | tf_op jit(solution)/shard_map/ppermute | solution.py:162
  473.9 6.0 collective-permute-done.73
  481.4 9.2 %collective-permute-done.74 = bf16[128,1280]{1,0:T(8,128)(2,1)S(1)} collective-permute-done((bf16[128,1280]{1,0:T(8,128)(2,1)S(1)}, bf16[128,1280]{1,0:T(8,128)(2,1)S(1)}, u32[]{:S(2)}, u32[]{:S(2)}) %collective-permute-start.74) | collective-permute-done | bytes 327712 | tf_op jit(solution)/shard_map/ppermute | solution.py:162
  522.7 6.1 collective-permute-start.33
  545.7 26.6 %collective-permute-done.43 = bf16[128,1152]{1,0:T(8,128)(2,1)S(1)} collective-permute-done((bf16[128,1152]{1,0:T(8,128)(2,1)S(1)}, bf16[128,1152]{1,0:T(8,128)(2,1)S(1)}, u32[]{:S(2)}, u32[]{:S(2)}) %collective-permute-start.43) | collective-permute-done | bytes 294944 | tf_op jit(solution)/shard_map/ppermute | solution.py:162
  605.8 5.1 collective-permute-done.25
  612.1 11.4 %collective-permute-done.55 = bf16[768,512]{1,0:T(8,128)(2,1)S(1)} collective-permute-done((bf16[768,512]{1,0:T(8,128)(2,1)S(1)}, bf16[768,512]{1,0:T(8,128)(2,1)S(1)}, u32[]{:S(2)}, u32[]{:S(2)}) %collective-permute-start.55) | collective-permute-done | bytes 786464 | tf_op jit(solution)/shard_map/ppermute | solution.py:162
  625.5 14.0 %collective-permute-done.26 = bf16[4,96,384]{2,1,0:T(8,128)(2,1)S(1)} collective-permute-done((bf16[4,96,384]{2,1,0:T(8,128)(2,1)S(1)}, bf16[4,96,384]{2,1,0:T(8,128)(2,1)S(1)}, u32[]{:S(2)}, u32[]{:S(2)}) %collective-permute-start.26) | collective-permute-done | bytes 294944 | tf_op jit(solution)/shard_map/ppermute | solution.py:162
  650.2 10.8 %collective-permute-done.28 = bf16[1,96,384]{2,1,0:T(8,128)(2,1)S(1)} collective-permute-done((bf16[1,96,384]{2,1,0:T(8,128)(2,1)S(1)}, bf16[1,96,384]{2,1,0:T(8,128)(2,1)S(1)}, u32[]{:S(2)}, u32[]{:S(2)}) %collective-permute-start.28) | collective-permute-done | bytes 73760 | tf_op jit(solution)/shard_map/ppermute | solution.py:162
  663.2 3.9 collective-permute-start.59
  667.8 19.9 %collective-permute-done.58 = bf16[1,96,512]{2,1,0:T(8,128)(2,1)S(1)} collective-permute-done((bf16[1,96,512]{2,1,0:T(8,128)(2,1)S(1)}, bf16[1,96,512]{2,1,0:T(8,128)(2,1)S(1)}, u32[]{:S(2)}, u32[]{:S(2)}) %collective-permute-start.58) | collective-permute-done | bytes 98336 | tf_op jit(solution)/shard_map/ppermute | solution.py:162
  (978 shorter events, 439.7 us)
Async XLA Ops:
  15.6 39.1 %collective-permute-start.2 = (bf16[64,1664]{1,0:T(8,128)(2,1)}, bf16[64,1664]{1,0:T(8,128)(2,1)}, u32[]{:S(2)}, u32[]{:S(2)}) collective-permute-start(bf16[64,1664]{1,0:T(8,128)(2,1)} %get-tuple-element.165), channel_id=1, source_target_pairs={{0,1},{1,0},{2,3},{3,2},{4,5},{5,4},{6,7},{7,6},{8,9},{9,8},{10,11... | collective-permute-start | bytes 638984 | tf_op jit(solution)/shard_map/ppermute | solution.py:162
  24.0 42.3 %collective-permute-start = (bf16[128,1536]{1,0:T(8,128)(2,1)}, bf16[128,1536]{1,0:T(8,128)(2,1)}, u32[]{:S(2)}, u32[]{:S(2)}) collective-permute-start(bf16[128,1536]{1,0:T(8,128)(2,1)} %get-tuple-element.123), channel_id=1, source_target_pairs={{0,1},{1,2},{2,3},{3,4},{4,5},{5,6},{6,7},{8,9},{9,10},{10,11},{11... | collective-permute-start | bytes 1179656 | tf_op jit(solution)/shard_map/ppermute | solution.py:24
  26.7 39.6 %collective-permute-start.1 = (bf16[128,1536]{1,0:T(8,128)(2,1)}, bf16[128,1536]{1,0:T(8,128)(2,1)}, u32[]{:S(2)}, u32[]{:S(2)}) collective-permute-start(bf16[128,1536]{1,0:T(8,128)(2,1)} %get-tuple-element.124), channel_id=1, source_target_pairs={{1,0},{2,1},{3,2},{4,3},{5,4},{6,5},{7,6},{9,8},{10,9},{11,10},{12... | collective-permute-start | bytes 1179656 | tf_op jit(solution)/shard_map/ppermute | solution.py:26
  56.3 37.8 %collective-permute-start.3 = (bf16[128,1664]{1,0:T(8,128)(2,1)}, bf16[128,1664]{1,0:T(8,128)(2,1)}, u32[]{:S(2)}, u32[]{:S(2)}) collective-permute-start(bf16[128,1664]{1,0:T(8,128)(2,1)} %pad_maximum_fusion.11), channel_id=1, source_target_pairs={{0,2},{1,3},{2,4},{3,5},{4,6},{5,7},{6,0},{7,1},{8,10},{9,11},{10,... | collective-permute-start | bytes 1277960 | tf_op jit(solution)/shard_map/ppermute | solution.py:162
  60.7 34.5 %collective-permute-start.4 = (bf16[128,1664]{1,0:T(8,128)(2,1)}, bf16[128,1664]{1,0:T(8,128)(2,1)}, u32[]{:S(2)}, u32[]{:S(2)}) collective-permute-start(bf16[128,1664]{1,0:T(8,128)(2,1)} %pad_maximum_fusion.11), channel_id=1, source_target_pairs={{0,4},{1,5},{2,6},{3,7},{4,0},{5,1},{6,2},{7,3},{8,12},{9,13},{10,... | collective-permute-start | bytes 1277960 | tf_op jit(solution)/shard_map/ppermute | solution.py:162
  63.3 33.0 %collective-permute-start.5 = (bf16[128,1664]{1,0:T(8,128)(2,1)}, bf16[128,1664]{1,0:T(8,128)(2,1)}, u32[]{:S(2)}, u32[]{:S(2)}) collective-permute-start(bf16[128,1664]{1,0:T(8,128)(2,1)} %pad_maximum_fusion.11), channel_id=1, source_target_pairs={{0,6},{1,7},{2,0},{3,1},{4,2},{5,3},{6,4},{7,5},{8,14},{9,15},{10,... | collective-permute-start | bytes 1277960 | tf_op jit(solution)/shard_map/ppermute | solution.py:162
  197.2 111.7 %collective-permute-start.6 = (bf16[64,1664]{1,0:T(8,128)(2,1)S(1)}, bf16[64,1664]{1,0:T(8,128)(2,1)}, u32[]{:S(2)}, u32[]{:S(2)}) collective-permute-start(bf16[64,1664]{1,0:T(8,128)(2,1)S(1)} %concatenate.177), channel_id=1, source_target_pairs={{0,1},{1,0},{2,3},{3,2},{4,5},{5,4},{6,7},{7,6},{8,9},{9,8},{10,11... | collective-permute-start | bytes 638984 | tf_op jit(solution)/shard_map/ppermute | solution.py:162
  253.8 59.9 %collective-permute-start.72 = (bf16[64,2816]{1,0:T(8,128)(2,1)}, bf16[64,2816]{1,0:T(8,128)(2,1)}, u32[]{:S(2)}, u32[]{:S(2)}) collective-permute-start(bf16[64,2816]{1,0:T(8,128)(2,1)} %pad_maximum_fusion.14), channel_id=1, source_target_pairs={{0,1},{1,0},{2,3},{3,2},{4,5},{5,4},{6,7},{7,6},{8,9},{9,8},{10,11... | collective-permute-start | bytes 1081352 | tf_op jit(solution)/shard_map/ppermute | solution.py:162
  262.5 121.2 %collective-permute-start.66 = (bf16[64,4864]{1,0:T(8,128)(2,1)}, bf16[64,4864]{1,0:T(8,128)(2,1)}, u32[]{:S(2)}, u32[]{:S(2)}) collective-permute-start(bf16[64,4864]{1,0:T(8,128)(2,1)} %pad_maximum_fusion.9), channel_id=1, source_target_pairs={{0,8},{8,0},{16,24},{24,16},{1,9},{9,1},{17,25},{25,17},{2,10},{10... | collective-permute-start | bytes 1867784 | tf_op jit(solution)/shard_map/ppermute | solution.py:162
  274.4 23.7 %collective-permute-start.48 = (bf16[64,1152]{1,0:T(8,128)(2,1)}, bf16[64,1152]{1,0:T(8,128)(2,1)}, u32[]{:S(2)}, u32[]{:S(2)}) collective-permute-start(bf16[64,1152]{1,0:T(8,128)(2,1)} %pad_maximum_fusion.26), channel_id=1, source_target_pairs={{0,8},{8,0},{16,24},{24,16},{1,9},{9,1},{17,25},{25,17},{2,10},{10... | collective-permute-start | bytes 442376 | tf_op jit(solution)/shard_map/ppermute | solution.py:162
  277.1 22.4 %collective-permute-start.36 = (bf16[64,1152]{1,0:T(8,128)(2,1)}, bf16[64,1152]{1,0:T(8,128)(2,1)}, u32[]{:S(2)}, u32[]{:S(2)}) collective-permute-start(bf16[64,1152]{1,0:T(8,128)(2,1)} %pad_maximum_fusion.25), channel_id=1, source_target_pairs={{0,8},{8,0},{16,24},{24,16},{1,9},{9,1},{17,25},{25,17},{2,10},{10... | collective-permute-start | bytes 442376 | tf_op jit(solution)/shard_map/ppermute | solution.py:162
  298.0 78.0 %collective-permute-start.30 = (bf16[2,768,192]{1,2,0:T(8,128)(2,1)}, bf16[2,768,192]{1,2,0:T(8,128)(2,1)}, u32[]{:S(2)}, u32[]{:S(2)}) collective-permute-start(bf16[2,768,192]{1,2,0:T(8,128)(2,1)} %dynamic-slice_bitcast_fusion.3), channel_id=1, source_target_pairs={{0,8},{8,0},{16,24},{24,16},{1,9},{9,1},{17,25},{25,17},{2,10},{10... | collective-permute-start | bytes 1769480 | tf_op jit(solution)/shard_map/ppermute | solution.py:162
  313.7 21.4 %collective-permute-start.49 = (bf16[128,960]{1,0:T(8,128)(2,1)}, bf16[128,960]{1,0:T(8,128)(2,1)}, u32[]{:S(2)}, u32[]{:S(2)}) collective-permute-start(bf16[128,960]{1,0:T(8,128)(2,1)} %pad_maximum_fusion.21), channel_id=1, source_target_pairs={{0,16},{8,24},{16,0},{24,8},{1,17},{9,25},{17,1},{25,9},{2,18},{10... | collective-permute-start | bytes 737288 | tf_op jit(solution)/shard_map/ppermute | solution.py:162
  319.7 27.3 %collective-permute-start.37 = (bf16[128,960]{1,0:T(8,128)(2,1)}, bf16[128,960]{1,0:T(8,128)(2,1)}, u32[]{:S(2)}, u32[]{:S(2)}) collective-permute-start(bf16[128,960]{1,0:T(8,128)(2,1)} %pad_maximum_fusion.20), channel_id=1, source_target_pairs={{0,16},{8,24},{16,0},{24,8},{1,17},{9,25},{17,1},{25,9},{2,18},{10... | collective-permute-start | bytes 737288 | tf_op jit(solution)/shard_map/ppermute | solution.py:162
  373.4 121.8 %collective-permute-start.60 = (bf16[2,1024,192]{1,2,0:T(8,128)(2,1)}, bf16[2,1024,192]{1,2,0:T(8,128)(2,1)}, u32[]{:S(2)}, u32[]{:S(2)}) collective-permute-start(bf16[2,1024,192]{1,2,0:T(8,128)(2,1)} %dynamic-slice_bitcast_fusion.2), channel_id=1, source_target_pairs={{0,8},{8,0},{16,24},{24,16},{1,9},{9,1},{17,25},{25,17},{2,10},{10... | collective-permute-start | bytes 2359304 | tf_op jit(solution)/shard_map/ppermute | solution.py:162
  374.4 220.1 %collective-permute-start.54 = (bf16[2,768,512]{2,1,0:T(8,128)(2,1)}, bf16[2,768,512]{2,1,0:T(8,128)(2,1)}, u32[]{:S(2)}, u32[]{:S(2)}) collective-permute-start(bf16[2,768,512]{2,1,0:T(8,128)(2,1)} %dynamic-slice_bitcast_fusion), channel_id=1, source_target_pairs={{0,8},{8,0},{16,24},{24,16},{1,9},{9,1},{17,25},{25,17},{2,10},{10... | collective-permute-start | bytes 4718600 | tf_op jit(solution)/shard_map/ppermute | solution.py:162
  378.8 29.7 %collective-permute-start.8 = (bf16[128,1664]{1,0:T(8,128)(2,1)S(1)}, bf16[128,1664]{1,0:T(8,128)(2,1)S(1)}, u32[]{:S(2)}, u32[]{:S(2)}) collective-permute-start(bf16[128,1664]{1,0:T(8,128)(2,1)S(1)} %copy-done.135), channel_id=1, source_target_pairs={{0,4},{1,5},{2,6},{3,7},{4,0},{5,1},{6,2},{7,3},{8,12},{9,13},{10,... | collective-permute-start | bytes 1277960 | tf_op jit(solution)/shard_map/ppermute | solution.py:162
  383.7 25.6 %collective-permute-start.9 = (bf16[128,1664]{1,0:T(8,128)(2,1)S(1)}, bf16[128,1664]{1,0:T(8,128)(2,1)S(1)}, u32[]{:S(2)}, u32[]{:S(2)}) collective-permute-start(bf16[128,1664]{1,0:T(8,128)(2,1)S(1)} %copy-done.135), channel_id=1, source_target_pairs={{0,6},{1,7},{2,0},{3,1},{4,2},{5,3},{6,4},{7,5},{8,14},{9,15},{10,... | collective-permute-start | bytes 1277960 | tf_op jit(solution)/shard_map/ppermute | solution.py:162
  469.9 22.2 %collective-permute-start.75 = (bf16[128,1280]{1,0:T(8,128)(2,1)S(1)}, bf16[128,1280]{1,0:T(8,128)(2,1)S(1)}, u32[]{:S(2)}, u32[]{:S(2)}) collective-permute-start(bf16[128,1280]{1,0:T(8,128)(2,1)S(1)} %copy-done.142), channel_id=1, source_target_pairs={{0,6},{1,7},{2,0},{3,1},{4,2},{5,3},{6,4},{7,5},{8,14},{9,15},{10,... | collective-permute-start | bytes 983048 | tf_op jit(solution)/shard_map/ppermute | solution.py:162
  495.4 47.2 %collective-permute-start.76 = (bf16[2,512,192]{1,2,0:T(8,128)(2,1)}, bf16[2,512,192]{1,2,0:T(8,128)(2,1)}, u32[]{:S(2)}, u32[]{:S(2)}) collective-permute-start(bf16[2,512,192]{1,2,0:T(8,128)(2,1)} %dynamic-slice_bitcast_fusion.5), channel_id=1, source_target_pairs={{0,8},{8,0},{16,24},{24,16},{1,9},{9,1},{17,25},{25,17},{2,10},{10... | collective-permute-start | bytes 1179656 | tf_op jit(solution)/shard_map/ppermute | solution.py:162
  538.8 53.4 %collective-permute-start.24 = (bf16[2,768,384]{2,1,0:T(8,128)(2,1)}, bf16[2,768,384]{2,1,0:T(8,128)(2,1)}, u32[]{:S(2)}, u32[]{:S(2)}) collective-permute-start(bf16[2,768,384]{2,1,0:T(8,128)(2,1)} %dynamic-slice_bitcast_fusion.1), channel_id=1, source_target_pairs={{0,8},{8,0},{16,24},{24,16},{1,9},{9,1},{17,25},{25,17},{2,10},{10... | collective-permute-start | bytes 3538952 | tf_op jit(solution)/shard_map/ppermute | solution.py:162
  539.9 42.8 %collective-permute-start.67 = (bf16[128,2816]{1,0:T(8,128)(2,1)}, bf16[128,2816]{1,0:T(8,128)(2,1)}, u32[]{:S(2)}, u32[]{:S(2)}) collective-permute-start(bf16[128,2816]{1,0:T(8,128)(2,1)} %pad_maximum_fusion.8), channel_id=1, source_target_pairs={{0,16},{8,24},{16,0},{24,8},{1,17},{9,25},{17,1},{25,9},{2,18},{10... | collective-permute-start | bytes 2162696 | tf_op jit(solution)/shard_map/ppermute | solution.py:162
  541.1 33.4 %collective-permute-start.61 = (bf16[1024,192]{0,1:T(8,128)(2,1)S(1)}, bf16[1024,192]{0,1:T(8,128)(2,1)S(1)}, u32[]{:S(2)}, u32[]{:S(2)}) collective-permute-start(bf16[1024,192]{0,1:T(8,128)(2,1)S(1)} %copy-done.141), channel_id=1, source_target_pairs={{0,16},{8,24},{16,0},{24,8},{1,17},{9,25},{17,1},{25,9},{2,18},{10... | collective-permute-start | bytes 1179656 | tf_op jit(solution)/shard_map/ppermute | solution.py:162
  542.6 29.7 %collective-permute-start.43 = (bf16[128,1152]{1,0:T(8,128)(2,1)S(1)}, bf16[128,1152]{1,0:T(8,128)(2,1)S(1)}, u32[]{:S(2)}, u32[]{:S(2)}) collective-permute-start(bf16[128,1152]{1,0:T(8,128)(2,1)S(1)} %copy-done.148), channel_id=1, source_target_pairs={{0,16},{8,24},{16,0},{24,8},{1,17},{9,25},{17,1},{25,9},{2,18},{10... | collective-permute-start | bytes 884744 | tf_op jit(solution)/shard_map/ppermute | solution.py:162
  604.1 40.1 %collective-permute-start.68 = (bf16[256,2432]{1,0:T(8,128)(2,1)S(1)}, bf16[256,2432]{1,0:T(8,128)(2,1)S(1)}, u32[]{:S(2)}, u32[]{:S(2)}) collective-permute-start(bf16[256,2432]{1,0:T(8,128)(2,1)S(1)} %maximum_maximum_fusion), channel_id=1, source_target_pairs={{0,1},{1,0},{2,3},{3,2},{4,5},{5,4},{6,7},{7,6},{8,9},{9,8},{10,11... | collective-permute-start | bytes 3735560 | tf_op jit(solution)/shard_map/ppermute | solution.py:162
  611.1 28.5 %collective-permute-start.26 = (bf16[4,96,384]{2,1,0:T(8,128)(2,1)S(1)}, bf16[4,96,384]{2,1,0:T(8,128)(2,1)S(1)}, u32[]{:S(2)}, u32[]{:S(2)}) collective-permute-start(bf16[4,96,384]{2,1,0:T(8,128)(2,1)S(1)} %fusion.150), channel_id=1, source_target_pairs={{0,1},{1,0},{2,3},{3,2},{4,5},{5,4},{6,7},{7,6},{8,9},{9,8},{10,11... | collective-permute-start | bytes 884744 | tf_op jit(solution)/shard_map/ppermute | solution.py:162
  623.8 21.6 %collective-permute-start.56 = (bf16[4,96,512]{2,1,0:T(8,128)(2,1)S(1)}, bf16[4,96,512]{2,1,0:T(8,128)(2,1)S(1)}, u32[]{:S(2)}, u32[]{:S(2)}) collective-permute-start(bf16[4,96,512]{2,1,0:T(8,128)(2,1)S(1)} %fusion.122), channel_id=1, source_target_pairs={{0,1},{1,0},{2,3},{3,2},{4,5},{5,4},{6,7},{7,6},{8,9},{9,8},{10,11... | collective-permute-start | bytes 1179656 | tf_op jit(solution)/shard_map/ppermute | solution.py:162
  645.8 42.6 %collective-permute-start.69 = (bf16[1,96,2048]{2,1,0:T(8,128)(2,1)S(1)}, bf16[1,96,2048]{2,1,0:T(8,128)(2,1)S(1)}, u32[]{:S(2)}, u32[]{:S(2)}) collective-permute-start(bf16[1,96,2048]{2,1,0:T(8,128)(2,1)S(1)} %get-tuple-element.102), channel_id=1, source_target_pairs={{0,2},{1,3},{2,4},{3,5},{4,6},{5,7},{6,0},{7,1},{8,10},{9,11},{10,... | collective-permute-start | bytes 1179656 | tf_op jit(solution)/shard_map/ppermute | solution.py:162
  647.8 40.6 %collective-permute-start.70 = (bf16[1,96,2048]{2,1,0:T(8,128)(2,1)S(1)}, bf16[1,96,2048]{2,1,0:T(8,128)(2,1)S(1)}, u32[]{:S(2)}, u32[]{:S(2)}) collective-permute-start(bf16[1,96,2048]{2,1,0:T(8,128)(2,1)S(1)} %get-tuple-element.104), channel_id=1, source_target_pairs={{0,4},{1,5},{2,6},{3,7},{4,0},{5,1},{6,2},{7,3},{8,12},{9,13},{10,... | collective-permute-start | bytes 1179656 | tf_op jit(solution)/shard_map/ppermute | solution.py:162
  661.0 27.4 %collective-permute-start.71 = (bf16[1,96,2048]{2,1,0:T(8,128)(2,1)S(1)}, bf16[1,96,2048]{2,1,0:T(8,128)(2,1)S(1)}, u32[]{:S(2)}, u32[]{:S(2)}) collective-permute-start(bf16[1,96,2048]{2,1,0:T(8,128)(2,1)S(1)} %get-tuple-element.103), channel_id=1, source_target_pairs={{0,6},{1,7},{2,0},{3,1},{4,2},{5,3},{6,4},{7,5},{8,14},{9,15},{10,... | collective-permute-start | bytes 1179656 | tf_op jit(solution)/shard_map/ppermute | solution.py:162
  661.0 26.6 %collective-permute-start.58 = (bf16[1,96,512]{2,1,0:T(8,128)(2,1)S(1)}, bf16[1,96,512]{2,1,0:T(8,128)(2,1)S(1)}, u32[]{:S(2)}, u32[]{:S(2)}) collective-permute-start(bf16[1,96,512]{2,1,0:T(8,128)(2,1)S(1)} %get-tuple-element.131), channel_id=1, source_target_pairs={{0,4},{1,5},{2,6},{3,7},{4,0},{5,1},{6,2},{7,3},{8,12},{9,13},{10,... | collective-permute-start | bytes 294920 | tf_op jit(solution)/shard_map/ppermute | solution.py:162
  663.2 24.5 %collective-permute-start.59 = (bf16[1,96,512]{2,1,0:T(8,128)(2,1)S(1)}, bf16[1,96,512]{2,1,0:T(8,128)(2,1)S(1)}, u32[]{:S(2)}, u32[]{:S(2)}) collective-permute-start(bf16[1,96,512]{2,1,0:T(8,128)(2,1)S(1)} %get-tuple-element.130), channel_id=1, source_target_pairs={{0,6},{1,7},{2,0},{3,1},{4,2},{5,3},{6,4},{7,5},{8,14},{9,15},{10,... | collective-permute-start | bytes 294920 | tf_op jit(solution)/shard_map/ppermute | solution.py:162
  (284 other events, 2720.5 us)
